TPU v7x, 32 devices: a whole 2x2x4 slice. The times are simulated.
32 devices in a mesh: dp: 16 (over z, y, core), inner: 2 (over x).
Axes of the slice: x: 2, y: 2, z: 4, core: 2. Of those that a mesh axis runs over, the one named last changes fastest.
Arguments:
- target: bfloat16 [32, 1024, 512], P(('dp', 'inner')), may hold values from -6 to 6
- source: bfloat16 [32, 344, 512], P(('dp', 'inner')), may hold values from -6 to 6
- target_segment: int32 [32, 1024], P(('dp', 'inner')), may hold values from 0 to 11, as said below
- source_segment: int32 [32, 344], P(('dp', 'inner')), may hold values from 0 to 11, as said below
- source_keep: int32 [32, 344], P(('dp', 'inner')), may hold values from 0 to 1, as said below
- self_query: bfloat16 [512, 512], P('dp', 'inner'), may hold values from -0.25 to 0.25
- self_key: bfloat16 [512, 512], P('dp', 'inner'), may hold values from -0.25 to 0.25
- self_value: bfloat16 [512, 512], P('dp', 'inner'), may hold values from -0.25 to 0.25
- self_output: bfloat16 [512, 512], P('dp', 'inner'), may hold values from -1 to 1
- cross_query: bfloat16 [512, 512], P('dp', 'inner'), may hold values from -0.25 to 0.25
- cross_key: bfloat16 [512, 512], P('dp', 'inner'), may hold values from -0.25 to 0.25
- cross_value: bfloat16 [512, 512], P('dp', 'inner'), may hold values from -0.25 to 0.25
- cross_output: bfloat16 [512, 512], P('dp', 'inner'), may hold values from -1 to 1
- expand_weight: bfloat16 [512, 2048], P('dp', 'inner'), may hold values from -0.25 to 0.25
- shrink_weight: bfloat16 [2048, 512], P('dp', 'inner'), may hold values from -0.125 to 0.125
- norm_affine: bfloat16 [6, 512], P('inner', 'dp'), may hold values from -2 to 2
- cotangent: bfloat16 [32, 1024, 512], P(('dp', 'inner')), may hold values from -6 to 6
Outputs:
- output: bfloat16 [32, 1024, 512], P(('dp', 'inner'))
- target_gradient: float32 [32, 1024, 512], P(('dp', 'inner'))
- source_gradient: float32 [32, 344, 512], P(('dp', 'inner'))
- self_query_gradient: float32 [512, 512], P('dp', 'inner')
- self_key_gradient: float32 [512, 512], P('dp', 'inner')
- self_value_gradient: float32 [512, 512], P('dp', 'inner')
- self_output_gradient: float32 [512, 512], P('dp', 'inner')
- cross_query_gradient: float32 [512, 512], P('dp', 'inner')
- cross_key_gradient: float32 [512, 512], P('dp', 'inner')
- cross_value_gradient: float32 [512, 512], P('dp', 'inner')
- cross_output_gradient: float32 [512, 512], P('dp', 'inner')
- expand_weight_gradient: float32 [512, 2048], P('dp', 'inner')
- shrink_weight_gradient: float32 [2048, 512], P('dp', 'inner')
- norm_affine_gradient: float32 [6, 512], P('inner', 'dp')
Inputs may be any that keep to these rules, and one draw needn't show every extreme that they name: In every row the numbers never fall, start at 0 and take every value up to 11; a row's documents appear in the same order in target_segment and source_segment. `source_segment`: same documents as target_segment; every document has at least one source position. `source_keep`: the first source position of every document is kept.
All inputs are finite; a program needn't handle non-finite values.
Results may differ from a plain program's by a relative error of at most 0.018.
Values may be sent and summed in bfloat16 or wider, within the bound.
No kernel may reach another device: no remote copies, remote signals or barrier semaphores. Data moves between devices by JAX's collectives and lax.ppermute only.
A program may use at most 192 MiB of HBM per device.

v0:
```python
import jax
import jax.numpy as jnp
from jax import lax
from jax.sharding import PartitionSpec as P

HEAD_DIM = 64
BLOCK = 512


EPS = 1e-05
NEG = -1e30


def layer_norm(stream, gain, bias):
    centre = stream - jnp.mean(stream, -1, keepdims=True)
    spread = jnp.mean(centre * centre, -1, keepdims=True)
    return centre * lax.rsqrt(spread + EPS) * gain + bias


def forward_dot(left, weight):
    return jnp.dot(left, weight, preferred_element_type=jnp.float32)


def weight_dot(left, right):
    return lax.dot_general(
        left, right, (((0,), (0,)), ((), ())), preferred_element_type=jnp.float32
    )


def input_dot(upstream, weight):
    return lax.dot_general(
        upstream, weight, (((1,), (1,)), ((), ())), preferred_element_type=jnp.float32
    )


def gather_all(w_sq, w_sk, w_sv, w_so, w_cq, w_ck, w_cv, w_co, expand, shrink, affine):
    halves = (
        lax.all_gather(w_sq, "inner", axis=1, tiled=True),
        lax.all_gather(w_sk, "inner", axis=1, tiled=True),
        lax.all_gather(w_sv, "inner", axis=1, tiled=True),
        lax.all_gather(w_so, "inner", axis=1, tiled=True),
        lax.all_gather(w_cq, "inner", axis=1, tiled=True),
        lax.all_gather(w_ck, "inner", axis=1, tiled=True),
        lax.all_gather(w_cv, "inner", axis=1, tiled=True),
        lax.all_gather(w_co, "inner", axis=1, tiled=True),
        lax.all_gather(expand, "inner", axis=1, tiled=True),
        lax.all_gather(shrink, "inner", axis=1, tiled=True),
        lax.all_gather(affine, "inner", axis=0, tiled=True),
    )
    return (
        lax.all_gather(halves[0], "dp", axis=0, tiled=True),
        lax.all_gather(halves[1], "dp", axis=0, tiled=True),
        lax.all_gather(halves[2], "dp", axis=0, tiled=True),
        lax.all_gather(halves[3], "dp", axis=0, tiled=True),
        lax.all_gather(halves[4], "dp", axis=0, tiled=True),
        lax.all_gather(halves[5], "dp", axis=0, tiled=True),
        lax.all_gather(halves[6], "dp", axis=0, tiled=True),
        lax.all_gather(halves[7], "dp", axis=0, tiled=True),
        lax.all_gather(halves[8], "dp", axis=0, tiled=True),
        lax.all_gather(halves[9], "dp", axis=0, tiled=True),
        lax.all_gather(halves[10], "dp", axis=1, tiled=True),
    )


def reduce_all(g_sq, g_sk, g_sv, g_so, g_cq, g_ck, g_cv, g_co, g_expand, g_shrink, g_affine):
    partial_sums = (
        lax.psum_scatter(g_sq, "dp", scatter_dimension=0, tiled=True),
        lax.psum_scatter(g_sk, "dp", scatter_dimension=0, tiled=True),
        lax.psum_scatter(g_sv, "dp", scatter_dimension=0, tiled=True),
        lax.psum_scatter(g_so, "dp", scatter_dimension=0, tiled=True),
        lax.psum_scatter(g_cq, "dp", scatter_dimension=0, tiled=True),
        lax.psum_scatter(g_ck, "dp", scatter_dimension=0, tiled=True),
        lax.psum_scatter(g_cv, "dp", scatter_dimension=0, tiled=True),
        lax.psum_scatter(g_co, "dp", scatter_dimension=0, tiled=True),
        lax.psum_scatter(g_expand, "dp", scatter_dimension=0, tiled=True),
        lax.psum_scatter(g_shrink, "dp", scatter_dimension=0, tiled=True),
        lax.psum_scatter(g_affine, "dp", scatter_dimension=1, tiled=True),
    )
    return (
        lax.psum_scatter(
            partial_sums[0].astype(jnp.bfloat16), "inner", scatter_dimension=1, tiled=True
        ).astype(jnp.float32),
        lax.psum_scatter(
            partial_sums[1].astype(jnp.bfloat16), "inner", scatter_dimension=1, tiled=True
        ).astype(jnp.float32),
        lax.psum_scatter(
            partial_sums[2].astype(jnp.bfloat16), "inner", scatter_dimension=1, tiled=True
        ).astype(jnp.float32),
        lax.psum_scatter(
            partial_sums[3].astype(jnp.bfloat16), "inner", scatter_dimension=1, tiled=True
        ).astype(jnp.float32),
        lax.psum_scatter(
            partial_sums[4].astype(jnp.bfloat16), "inner", scatter_dimension=1, tiled=True
        ).astype(jnp.float32),
        lax.psum_scatter(
            partial_sums[5].astype(jnp.bfloat16), "inner", scatter_dimension=1, tiled=True
        ).astype(jnp.float32),
        lax.psum_scatter(
            partial_sums[6].astype(jnp.bfloat16), "inner", scatter_dimension=1, tiled=True
        ).astype(jnp.float32),
        lax.psum_scatter(
            partial_sums[7].astype(jnp.bfloat16), "inner", scatter_dimension=1, tiled=True
        ).astype(jnp.float32),
        lax.psum_scatter(
            partial_sums[8].astype(jnp.bfloat16), "inner", scatter_dimension=1, tiled=True
        ).astype(jnp.float32),
        lax.psum_scatter(
            partial_sums[9].astype(jnp.bfloat16), "inner", scatter_dimension=1, tiled=True
        ).astype(jnp.float32),
        lax.psum_scatter(
            partial_sums[10].astype(jnp.bfloat16), "inner", scatter_dimension=0, tiled=True
        ).astype(jnp.float32),
    )


def pair_mask(query_segs, key_segs, keep_row):
    return (query_segs[:, None] == key_segs[None, :]) & (keep_row[None, :] > 0)


def pair_scores(query_block, key_rows, allowed):
    raw = (
        jnp.einsum("qhd,khd->hqk", query_block, key_rows, preferred_element_type=jnp.float32)
        * 0.125
    )
    return jnp.where(allowed[None], raw, NEG)


def slice_pair(array, row, column):
    count = array.shape[1]
    piece = lax.dynamic_slice(array, (row, 0, column), (1, count, 2 * HEAD_DIM))
    return piece[0].reshape(count, 2, HEAD_DIM)


def merge_heads(pieces, rows, count, width):
    pairs = width // (2 * HEAD_DIM)
    return (
        pieces.reshape(rows, pairs, count, 2 * HEAD_DIM)
        .transpose(0, 2, 1, 3)
        .reshape(rows, count, width)
    )


def attend(query, keys, values, query_segment, key_segment, key_keep):
    rows, length, width = query.shape
    pairs = width // (2 * HEAD_DIM)
    blocks = length // BLOCK

    def one_pair(index):
        row = index // pairs
        column = index % pairs * (2 * HEAD_DIM)
        query_rows = slice_pair(query, row, column)
        key_rows = slice_pair(keys, row, column)
        value_rows = slice_pair(values, row, column)
        query_segs = query_segment[row]
        key_segs = key_segment[row]
        keep_row = key_keep[row]
        mixed_parts = []
        total_parts = []
        for part in range(blocks):
            lower = part * BLOCK
            allowed = pair_mask(query_segs[lower : lower + BLOCK], key_segs, keep_row)
            scores = pair_scores(query_rows[lower : lower + BLOCK], key_rows, allowed)
            top = jnp.max(scores, -1, keepdims=True)
            expo = jnp.exp(scores - top)
            total = jnp.sum(expo, -1, keepdims=True)
            probs = (expo / total).astype(jnp.bfloat16)
            mixed = jnp.einsum(
                "hqk,khd->qhd", probs, value_rows, preferred_element_type=jnp.float32
            )
            mixed_parts.append(mixed.reshape(BLOCK, 2 * HEAD_DIM))
            total_parts.append((top + jnp.log(total))[:, :, 0])
        return (jnp.concatenate(mixed_parts, 0), jnp.concatenate(total_parts, 1))

    mixed, log_total = lax.map(one_pair, jnp.arange(rows * pairs, dtype=jnp.int32))
    return (merge_heads(mixed, rows, length, width), log_total)


def attend_back(query, keys, values, mixed_back, log_total, query_segment, key_segment, key_keep):
    rows, length, width = query.shape
    count = keys.shape[1]
    pairs = width // (2 * HEAD_DIM)
    blocks = length // BLOCK

    def one_pair(index):
        row = index // pairs
        column = index % pairs * (2 * HEAD_DIM)
        query_rows = slice_pair(query, row, column)
        key_rows = slice_pair(keys, row, column)
        value_rows = slice_pair(values, row, column)
        back_rows = slice_pair(mixed_back, row, column)
        totals = log_total[index]
        query_segs = query_segment[row]
        key_segs = key_segment[row]
        keep_row = key_keep[row]
        key_total = jnp.zeros((count, 2, HEAD_DIM), jnp.float32)
        value_total = jnp.zeros((count, 2, HEAD_DIM), jnp.float32)
        query_parts = []
        for part in range(blocks):
            lower = part * BLOCK
            query_block = query_rows[lower : lower + BLOCK]
            back_block = back_rows[lower : lower + BLOCK]
            allowed = pair_mask(query_segs[lower : lower + BLOCK], key_segs, keep_row)
            scores = pair_scores(query_block, key_rows, allowed)
            probs = jnp.exp(scores - totals[:, lower : lower + BLOCK, None])
            value_total = value_total + jnp.einsum(
                "hqk,qhd->khd",
                probs.astype(jnp.bfloat16),
                back_block,
                preferred_element_type=jnp.float32,
            )
            spread_back = jnp.einsum(
                "qhd,khd->hqk", back_block, value_rows, preferred_element_type=jnp.float32
            )
            score_back = (
                probs * (spread_back - jnp.sum(probs * spread_back, -1, keepdims=True))
            ).astype(jnp.bfloat16)
            query_part = (
                jnp.einsum("hqk,khd->qhd", score_back, key_rows, preferred_element_type=jnp.float32)
                * 0.125
            )
            query_parts.append(query_part.reshape(BLOCK, 2 * HEAD_DIM))
            key_total = (
                key_total
                + jnp.einsum(
                    "hqk,qhd->khd", score_back, query_block, preferred_element_type=jnp.float32
                )
                * 0.125
            )
        return (
            jnp.concatenate(query_parts, 0),
            key_total.reshape(count, 2 * HEAD_DIM),
            value_total.reshape(count, 2 * HEAD_DIM),
        )

    query_back, key_back, value_back = lax.map(one_pair, jnp.arange(rows * pairs, dtype=jnp.int32))
    return (
        merge_heads(query_back, rows, length, width),
        merge_heads(key_back, rows, count, width),
        merge_heads(value_back, rows, count, width),
    )


def shards(
    target,
    source,
    target_segment,
    source_segment,
    source_keep,
    self_query,
    self_key,
    self_value,
    self_output,
    cross_query,
    cross_key,
    cross_value,
    cross_output,
    expand_weight,
    shrink_weight,
    norm_affine,
    cotangent,
):
    rows, length, width = target.shape
    src_length = source.shape[1]
    tokens = rows * length
    fetched = gather_all(
        self_query,
        self_key,
        self_value,
        self_output,
        cross_query,
        cross_key,
        cross_value,
        cross_output,
        expand_weight,
        shrink_weight,
        norm_affine,
    )
    w_sq, w_sk, w_sv, w_so, w_cq, w_ck, w_cv, w_co, expand, shrink, affine_low = fetched
    affine = affine_low.astype(jnp.float32)
    all_keep = jnp.ones_like(target_segment)
    stream = target.reshape(tokens, width).astype(jnp.float32)
    normed_one, norm_one_pull = jax.vjp(layer_norm, stream, affine[0], affine[1])
    normed_one = normed_one.astype(jnp.bfloat16)
    query = forward_dot(normed_one, w_sq).astype(jnp.bfloat16).reshape(rows, length, width)
    keys = forward_dot(normed_one, w_sk).astype(jnp.bfloat16).reshape(rows, length, width)
    values = forward_dot(normed_one, w_sv).astype(jnp.bfloat16).reshape(rows, length, width)
    self_mixed, self_total = attend(query, keys, values, target_segment, target_segment, all_keep)
    self_mixed = self_mixed.reshape(tokens, width).astype(jnp.bfloat16)
    first_sum = stream + forward_dot(self_mixed, w_so)
    normed_two, norm_two_pull = jax.vjp(layer_norm, first_sum, affine[2], affine[3])
    normed_two = normed_two.astype(jnp.bfloat16)
    encoded = source.reshape(rows * src_length, width)
    cross_q = forward_dot(normed_two, w_cq).astype(jnp.bfloat16).reshape(rows, length, width)
    cross_k = forward_dot(encoded, w_ck).astype(jnp.bfloat16).reshape(rows, src_length, width)
    cross_v = forward_dot(encoded, w_cv).astype(jnp.bfloat16).reshape(rows, src_length, width)
    cross_mixed, cross_total = attend(
        cross_q, cross_k, cross_v, target_segment, source_segment, source_keep
    )
    cross_mixed = cross_mixed.reshape(tokens, width).astype(jnp.bfloat16)
    second_sum = first_sum + forward_dot(cross_mixed, w_co)
    normed_three, norm_three_pull = jax.vjp(layer_norm, second_sum, affine[4], affine[5])
    normed_three = normed_three.astype(jnp.bfloat16)
    hidden = forward_dot(normed_three, expand)
    active, gelu_pull = jax.vjp(jax.nn.gelu, hidden)
    active = active.astype(jnp.bfloat16)
    result = (second_sum + forward_dot(active, shrink)).astype(jnp.bfloat16)
    refetched = gather_all(
        self_query,
        self_key,
        self_value,
        self_output,
        cross_query,
        cross_key,
        cross_value,
        cross_output,
        expand_weight,
        shrink_weight,
        norm_affine,
    )
    b_sq, b_sk, b_sv, b_so, b_cq, b_ck, b_cv, b_co, b_expand, b_shrink, b_affine = refetched
    out_back = cotangent.reshape(tokens, width)
    shrink_grad = weight_dot(active, out_back)
    active_back = input_dot(out_back, b_shrink)
    hidden_back = gelu_pull(active_back)[0].astype(jnp.bfloat16)
    expand_grad = weight_dot(normed_three, hidden_back)
    normed_three_back = input_dot(hidden_back, b_expand)
    second_ln, gain_three, bias_three = norm_three_pull(normed_three_back)
    second_back = out_back.astype(jnp.float32) + second_ln
    second_low = second_back.astype(jnp.bfloat16)
    cross_out_grad = weight_dot(cross_mixed, second_low)
    cross_mixed_back = input_dot(second_low, b_co).astype(jnp.bfloat16).reshape(rows, length, width)
    cq_back, ck_back, cv_back = attend_back(
        cross_q,
        cross_k,
        cross_v,
        cross_mixed_back,
        cross_total,
        target_segment,
        source_segment,
        source_keep,
    )
    cq_back = cq_back.reshape(tokens, width).astype(jnp.bfloat16)
    ck_back = ck_back.reshape(rows * src_length, width).astype(jnp.bfloat16)
    cv_back = cv_back.reshape(rows * src_length, width).astype(jnp.bfloat16)
    cross_query_grad = weight_dot(normed_two, cq_back)
    cross_key_grad = weight_dot(encoded, ck_back)
    cross_value_grad = weight_dot(encoded, cv_back)
    source_back = input_dot(ck_back, b_ck) + input_dot(cv_back, b_cv)
    normed_two_back = input_dot(cq_back, b_cq)
    first_ln, gain_two, bias_two = norm_two_pull(normed_two_back)
    first_back = second_back + first_ln
    first_low = first_back.astype(jnp.bfloat16)
    self_out_grad = weight_dot(self_mixed, first_low)
    self_mixed_back = input_dot(first_low, b_so).astype(jnp.bfloat16).reshape(rows, length, width)
    query_back, key_back, value_back = attend_back(
        query, keys, values, self_mixed_back, self_total, target_segment, target_segment, all_keep
    )
    query_back = query_back.reshape(tokens, width).astype(jnp.bfloat16)
    key_back = key_back.reshape(tokens, width).astype(jnp.bfloat16)
    value_back = value_back.reshape(tokens, width).astype(jnp.bfloat16)
    self_query_grad = weight_dot(normed_one, query_back)
    self_key_grad = weight_dot(normed_one, key_back)
    self_value_grad = weight_dot(normed_one, value_back)
    normed_one_back = (
        input_dot(query_back, b_sq) + input_dot(key_back, b_sk) + input_dot(value_back, b_sv)
    )
    stream_ln, gain_one, bias_one = norm_one_pull(normed_one_back)
    stream_back = first_back + stream_ln
    affine_grad = jnp.stack([gain_one, bias_one, gain_two, bias_two, gain_three, bias_three], 0)
    reduced = reduce_all(
        self_query_grad,
        self_key_grad,
        self_value_grad,
        self_out_grad,
        cross_query_grad,
        cross_key_grad,
        cross_value_grad,
        cross_out_grad,
        expand_grad,
        shrink_grad,
        affine_grad,
    )
    return (
        result.reshape(rows, length, width),
        stream_back.reshape(rows, length, width),
        source_back.reshape(rows, src_length, width),
        reduced[0],
        reduced[1],
        reduced[2],
        reduced[3],
        reduced[4],
        reduced[5],
        reduced[6],
        reduced[7],
        reduced[8],
        reduced[9],
        reduced[10],
    )


def solution(mesh):
    in_specs = (
        P(("dp", "inner"), None, None),
        P(("dp", "inner"), None, None),
        P(("dp", "inner"), None),
        P(("dp", "inner"), None),
        P(("dp", "inner"), None),
        P("dp", "inner"),
        P("dp", "inner"),
        P("dp", "inner"),
        P("dp", "inner"),
        P("dp", "inner"),
        P("dp", "inner"),
        P("dp", "inner"),
        P("dp", "inner"),
        P("dp", "inner"),
        P("dp", "inner"),
        P("inner", "dp"),
        P(("dp", "inner"), None, None),
    )
    out_specs = (
        P(("dp", "inner"), None, None),
        P(("dp", "inner"), None, None),
        P(("dp", "inner"), None, None),
        P("dp", "inner"),
        P("dp", "inner"),
        P("dp", "inner"),
        P("dp", "inner"),
        P("dp", "inner"),
        P("dp", "inner"),
        P("dp", "inner"),
        P("dp", "inner"),
        P("dp", "inner"),
        P("dp", "inner"),
        P("inner", "dp"),
    )
    return jax.shard_map(shards, mesh=mesh, in_specs=in_specs, out_specs=out_specs, check_vma=False)
```

profile of v0, /device:TPU:0, one launch (start us, length us, event | category | flops | bytes accessed | tf_op | source)
XLA Modules:
  0.0 1313.9 jit_solution(18239632158572571600)
XLA Ops:
  7.2 7.7 all_gather.104
  15.1 5.3 all_gather.106
  24.9 21.8 %all-gather.1 = bf16[16,32,6]{1,2,0:T(8,128)(2,1)S(1)} all-gather(bf16[1,32,6]{1,2,0:T(8,128)(2,1)S(1)} %bitcast.644), channel_id=1, replica_groups=mesh['dp'=16,'inner'=2] {'dp'}, dimensions={0}, use_global_device_ids=true | all-gather | bytes 6528 | tf_op jit(solution)/shard_map/all_gather | solution.py:61
  47.4 4.6 all_gather.90
  52.0 4.6 all_gather.92
  56.6 4.6 all_gather.88
  61.2 4.6 all_gather.94
  65.9 4.6 all_gather.98
  70.5 4.6 all_gather.100
  75.1 4.6 all_gather.96
  79.7 19.9 %all_gather.97 = bf16[512,512]{1,0:T(8,128)(2,1)S(1)} all-gather(bf16[32,512]{1,0:T(8,128)(2,1)S(1)} %all_gather.96), channel_id=1, replica_groups=mesh['dp'=16,'inner'=2] {'dp'}, dimensions={0}, use_global_device_ids=true | all-gather | bytes 557056 | tf_op jit(solution)/shard_map/all_gather | solution.py:57
  101.4 19.7 %all_gather.101 = bf16[512,512]{1,0:T(8,128)(2,1)S(1)} all-gather(bf16[32,512]{1,0:T(8,128)(2,1)S(1)} %all_gather.100), channel_id=1, replica_groups=mesh['dp'=16,'inner'=2] {'dp'}, dimensions={0}, use_global_device_ids=true | all-gather | bytes 557056 | tf_op jit(solution)/shard_map/all_gather | solution.py:56
  122.4 20.8 %all_gather.99 = bf16[512,512]{1,0:T(8,128)(2,1)} all-gather(bf16[32,512]{1,0:T(8,128)(2,1)S(1)} %all_gather.98), channel_id=1, replica_groups=mesh['dp'=16,'inner'=2] {'dp'}, dimensions={0}, use_global_device_ids=true | all-gather | bytes 557056 | tf_op jit(solution)/shard_map/all_gather | solution.py:55
  143.2 21.2 %all_gather.95 = bf16[512,512]{1,0:T(8,128)(2,1)} all-gather(bf16[32,512]{1,0:T(8,128)(2,1)S(1)} %all_gather.94), channel_id=1, replica_groups=mesh['dp'=16,'inner'=2] {'dp'}, dimensions={0}, use_global_device_ids=true | all-gather | bytes 557056 | tf_op jit(solution)/shard_map/all_gather | solution.py:54
  164.4 20.6 %all_gather.89 = bf16[512,512]{1,0:T(8,128)(2,1)} all-gather(bf16[32,512]{1,0:T(8,128)(2,1)S(1)} %all_gather.88), channel_id=1, replica_groups=mesh['dp'=16,'inner'=2] {'dp'}, dimensions={0}, use_global_device_ids=true | all-gather | bytes 557056 | tf_op jit(solution)/shard_map/all_gather | solution.py:53
  185.1 19.9 %all_gather.93 = bf16[512,512]{1,0:T(8,128)(2,1)S(1)} all-gather(bf16[32,512]{1,0:T(8,128)(2,1)S(1)} %all_gather.92), channel_id=1, replica_groups=mesh['dp'=16,'inner'=2] {'dp'}, dimensions={0}, use_global_device_ids=true | all-gather | bytes 557056 | tf_op jit(solution)/shard_map/all_gather | solution.py:52
  205.0 19.7 %all_gather.91 = bf16[512,512]{1,0:T(8,128)(2,1)S(1)} all-gather(bf16[32,512]{1,0:T(8,128)(2,1)S(1)} %all_gather.90), channel_id=1, replica_groups=mesh['dp'=16,'inner'=2] {'dp'}, dimensions={0}, use_global_device_ids=true | all-gather | bytes 557056 | tf_op jit(solution)/shard_map/all_gather | solution.py:51
  239.5 50.9 %while.60 = (s32[]{:T(128)}, bf16[4,1024,128]{1,2,0:T(8,128)(2,1)}, f32[4,2,1024]{2,1,0:T(2,128)S(1)}, s32[4]{0:T(128)S(1)}, bf16[1,1024,512]{1,2,0:T(8,128)(2,1...) while((s32[]{:T(128)}, bf16[4,1024,128]{1,2,0:T(8,128)(2,1)}, ...), condition=%wide.region_7.8_spmd, body=%wide.region_2.7_spmd.sunk | while | flops 563609600 | bytes 33128796 | solution.py:174
  301.6 33.7 %while.61 = (s32[]{:T(128)}, bf16[4,1024,128]{1,2,0:T(8,128)(2,1)}, f32[4,2,1024]{2,1,0:T(2,128)}, s32[4]{0:T(128)S(1)}, bf16[1,344,512]{1,2,0:T(8,128)(2,1)}, /...) while((s32[]{:T(128)}, bf16[4,1024,128]{1,2,0:T(8,128)(2,1)}, ...), condition=%wide.region_15.16_spmd, body=%wide.region_10.15_spmd.sunk | while | flops 187220320 | bytes 11536800 | solution.py:174
  337.6 4.6 all_gather.102
  342.3 20.1 %all_gather.103 = bf16[512,512]{1,0:T(8,128)(2,1)S(1)} all-gather(bf16[32,512]{1,0:T(8,128)(2,1)S(1)} %all_gather.102), channel_id=1, replica_groups=mesh['dp'=16,'inner'=2] {'dp'}, dimensions={0}, use_global_device_ids=true | all-gather | bytes 557056 | tf_op jit(solution)/shard_map/all_gather | solution.py:58
  366.3 8.1 fusion.100
  374.3 9.9 fusion.54
  400.3 92.2 %while.62 = (s32[]{:T(128)}, bf16[4,1024,128]{1,2,0:T(8,128)(2,1)}, bf16[4,344,128]{1,2,0:T(8,128)(2,1)}, bf16[4,344,128]{1,2,0:T(8,128)(2,1)}, s32[4]{0:T(128)S...) while((s32[]{:T(128)}, bf16[4,1024,128]{1,2,0:T(8,128)(2,1)}, ...), condition=%wide.region_23.24_spmd, body=%wide.region_20.23_spmd.sunk | while | flops 458937696 | bytes 29233528 | solution.py:235
  530.8 89.0 %while.63 = (s32[]{:T(128)}, bf16[4,1024,128]{1,2,0:T(8,128)(2,1)}, bf16[4,1024,128]{1,2,0:T(8,128)(2,1)}, bf16[4,1024,128]{1,2,0:T(8,128)(2,1)}, s32[4]{0:T(128...) while((s32[]{:T(128)}, bf16[4,1024,128]{1,2,0:T(8,128)(2,1)}, ...), condition=%wide.region_29.30_spmd, body=%wide.region_26.29_spmd.sunk | while | flops 1376122880 | bytes 76898712 | solution.py:235
  629.0 6.7 fusion.99
  636.9 9.1 fusion.84
  657.9 13.0 reduce-scatter.66.cloned.1.call-done
  672.6 58.7 %reduce-scatter.64.cloned.1.call-done = f32[32,512]{1,0:T(8,128)} async-done(((f32[512,512]{1,0:T(8,128)}), f32[32,512]{1,0:T(8,128)}) %reduce-scatter.64.cloned.1.call-update) | async-done | bytes 65552
  732.9 58.3 %reduce-scatter.40.cloned.1.call-done = f32[32,512]{1,0:T(8,128)} async-done(((f32[512,512]{1,0:T(8,128)}), f32[32,512]{1,0:T(8,128)}) %reduce-scatter.40.cloned.1.call-update) | async-done | bytes 65552 | tf_op jit(solution)/shard_map/reduce_scatter | solution.py:70
  794.0 57.8 %reduce-scatter.28.cloned.1.call-done = f32[32,512]{1,0:T(8,128)} async-done(((f32[512,512]{1,0:T(8,128)}), f32[32,512]{1,0:T(8,128)}) %reduce-scatter.28.cloned.1.call-update) | async-done | bytes 65552 | tf_op jit(solution)/shard_map/reduce_scatter | solution.py:67
  853.6 9.2 fusion.72
  862.8 49.0 %reduce-scatter.36.cloned.1.call-done = f32[32,512]{1,0:T(8,128)} async-done(((f32[512,512]{1,0:T(8,128)}), f32[32,512]{1,0:T(8,128)}) %reduce-scatter.36.cloned.1.call-update) | async-done | bytes 65552 | tf_op jit(solution)/shard_map/reduce_scatter | solution.py:69
  913.4 58.8 %reduce-scatter.32.cloned.1.call-done = f32[32,512]{1,0:T(8,128)} async-done(((f32[512,512]{1,0:T(8,128)}), f32[32,512]{1,0:T(8,128)}) %reduce-scatter.32.cloned.1.call-update) | async-done | bytes 65552 | tf_op jit(solution)/shard_map/reduce_scatter | solution.py:68
  981.6 66.0 %reduce-scatter.56.cloned.1.call-done = f32[32,2048]{1,0:T(8,128)} async-done(((f32[512,2048]{1,0:T(8,128)}), f32[32,2048]{1,0:T(8,128)}) %reduce-scatter.56.cloned.1.call-update) | async-done | bytes 262160 | tf_op jit(solution)/shard_map/reduce_scatter | solution.py:75
  1050.8 72.4 %reduce-scatter.60.cloned.1.call-done = f32[128,512]{1,0:T(8,128)} async-done(((f32[2048,512]{1,0:T(8,128)}), f32[128,512]{1,0:T(8,128)}) %reduce-scatter.60.cloned.1.call-update) | async-done | bytes 262160 | tf_op jit(solution)/shard_map/reduce_scatter | solution.py:76
  1126.1 55.0 %reduce-scatter.68.cloned.1.call-done = f32[32,6]{1,0:T(8,128)} async-done(((f32[512,6]{1,0:T(8,128)}), f32[32,6]{1,0:T(8,128)}) %reduce-scatter.68.cloned.1.call-update) | async-done | bytes 784
  1181.9 4.9 all-reduce
  1187.4 5.2 reduce-scatter.46.cloned.1.call-done
  1193.9 11.1 reduce-scatter.54.cloned.1.call-done
  1206.4 11.6 reduce-scatter.50.cloned.1.call-done
  1219.5 11.4 reduce-scatter.48.cloned.1.call-done
  1232.4 11.0 reduce-scatter.42.cloned.1.call-done
  1244.7 11.3 reduce-scatter.30.cloned.1.call-done
  1257.4 10.6 reduce-scatter.38.cloned.1.call-done
  1269.3 11.3 reduce-scatter.34.cloned.1.call-done
  1281.9 11.2 reduce-scatter.58.cloned.1.call-done
  1294.6 11.0 reduce-scatter.62.cloned.1.call-done
  (727 shorter events, 377.7 us)
Async XLA Ops:
  7.2 92.4 %copy-start = (bf16[1,344,512]{2,1,0:T(8,128)(2,1)S(1)}, bf16[1,344,512]{2,1,0:T(8,128)(2,1)}, u32[]{:S(2)}) copy-start(bf16[1,344,512]{2,1,0:T(8,128)(2,1)} %param.26) | copy-start | bytes 1056772
  7.2 359.1 %all-gather.5.cloned.1.call-start = ((), (), s32[]{:S(2)}) async-start(), calls=%async_computation.21 | async-start | bytes 2228224 | tf_op jit(solution)/shard_map/all_gather | solution.py:59
  15.0 359.3 %all-gather.7.cloned.1.call-start = ((), (), s32[]{:S(2)}) async-start(), calls=%async_computation.22 | async-start | bytes 2228224 | tf_op jit(solution)/shard_map/all_gather | solution.py:60
  20.3 634.4 %reduce-scatter.44.cloned.1.call-start = ((), (), s32[]{:S(2)}) async-start(), calls=%async_computation.31 | async-start | bytes 1114112 | tf_op jit(solution)/shard_map/reduce_scatter | solution.py:71
  47.4 185.7 %copy-start.63 = (f32[1,512]{1,0:T(1,128)}, f32[1,512]{1,0:T(1,128)S(1)}, u32[]{:S(2)}) copy-start(f32[1,512]{1,0:T(1,128)S(1)} %get-tuple-element.937) | copy-start | bytes 6148
  47.4 185.7 %copy-start.77 = (f32[1,512]{1,0:T(1,128)}, f32[1,512]{1,0:T(1,128)S(1)}, u32[]{:S(2)}) copy-start(f32[1,512]{1,0:T(1,128)S(1)} %get-tuple-element.936) | copy-start | bytes 6148
  47.4 246.8 %copy-start.61 = (f32[1,512]{1,0:T(1,128)}, f32[1,512]{1,0:T(1,128)S(1)}, u32[]{:S(2)}) copy-start(f32[1,512]{1,0:T(1,128)S(1)} %get-tuple-element.935) | copy-start | bytes 6148
  121.1 83.9 %copy-start.21 = (bf16[512,512]{1,0:T(8,128)(2,1)}, bf16[512,512]{1,0:T(8,128)(2,1)S(1)}, u32[]{:S(2)}) copy-start(bf16[512,512]{1,0:T(8,128)(2,1)S(1)} %all_gather.101) | copy-start | bytes 1572868
  121.1 103.6 %copy-start.41 = (bf16[1,1024,512]{2,1,0:T(8,128)(2,1)S(1)}, bf16[1,1024,512]{2,1,0:T(8,128)(2,1)}, u32[]{:S(2)}) copy-start(bf16[1,1024,512]{2,1,0:T(8,128)(2,1)} %param.25) | copy-start | bytes 3145732
  205.0 20.8 %copy-start.32 = (bf16[512,512]{1,0:T(8,128)(2,1)}, bf16[512,512]{1,0:T(8,128)(2,1)S(1)}, u32[]{:S(2)}) copy-start(bf16[512,512]{1,0:T(8,128)(2,1)S(1)} %all_gather.93) | copy-start | bytes 1572868
  224.7 5.0 copy-start.34
  225.4 7.7 copy-start.53
  225.7 7.4 copy-start.57
  364.6 30.4 %copy-start.59 = (f32[1024]{0:T(1024)}, f32[1024]{0:T(1024)S(1)}, u32[]{:S(2)}) copy-start(f32[1024]{0:T(1024)S(1)} %broadcast_multiply_fusion) | copy-start | bytes 12292
  366.2 28.8 %copy-start.72 = (f32[1024]{0:T(1024)}, f32[1024]{0:T(1024)S(1)}, u32[]{:S(2)}) copy-start(f32[1024]{0:T(1024)S(1)} %fusion.97) | copy-start | bytes 12292
  374.3 9.9 copy-start.81
  400.7 4.4 copy-start.46
  400.7 4.4 copy-start.83
  495.8 160.6 %reduce-scatter.52.cloned.1.call-start = ((), (), s32[]{:S(2)}) async-start(), calls=%async_computation.35 | async-start | bytes 1114112 | tf_op jit(solution)/shard_map/reduce_scatter | solution.py:74
  499.2 171.7 %reduce-scatter.66.cloned.1.call-start = ((), (), s32[]{:S(2)}) async-start(), calls=%async_computation.42 | async-start | bytes 1114112
  499.2 5.1 copy-start.54
  499.2 5.1 copy-start.58
  499.2 5.1 copy-start.64
  499.3 5.1 copy-start.78
  504.2 227.0 %reduce-scatter.64.cloned.1.call-start = ((), (), s32[]{:S(2)}) async-start(), calls=%async_computation.41 | async-start | bytes 1114112
  518.1 273.1 %reduce-scatter.40.cloned.1.call-start = ((), (), s32[]{:S(2)}) async-start(), calls=%async_computation.29 | async-start | bytes 1114112 | tf_op jit(solution)/shard_map/reduce_scatter | solution.py:70
  527.3 324.6 %reduce-scatter.28.cloned.1.call-start = ((), (), s32[]{:S(2)}) async-start(), calls=%async_computation.23 | async-start | bytes 1114112 | tf_op jit(solution)/shard_map/reduce_scatter | solution.py:67
  623.3 288.5 %reduce-scatter.36.cloned.1.call-start = ((), (), s32[]{:S(2)}) async-start(), calls=%async_computation.27 | async-start | bytes 1114112 | tf_op jit(solution)/shard_map/reduce_scatter | solution.py:69
  625.3 346.9 %reduce-scatter.32.cloned.1.call-start = ((), (), s32[]{:S(2)}) async-start(), calls=%async_computation.25 | async-start | bytes 1114112 | tf_op jit(solution)/shard_map/reduce_scatter | solution.py:68
  628.9 418.7 %reduce-scatter.56.cloned.1.call-start = ((), (), s32[]{:S(2)}) async-start(), calls=%async_computation.37 | async-start | bytes 4456448 | tf_op jit(solution)/shard_map/reduce_scatter | solution.py:75
  635.7 487.4 %reduce-scatter.60.cloned.1.call-start = ((), (), s32[]{:S(2)}) async-start(), calls=%async_computation.39 | async-start | bytes 4456448 | tf_op jit(solution)/shard_map/reduce_scatter | solution.py:76
  646.1 535.0 %reduce-scatter.68.cloned.1.call-start = ((), (), s32[]{:S(2)}) async-start(), calls=%async_computation.43 | async-start | bytes 278528
  652.9 139.9 %copy-start.82 = (u32[32]{0:T(128)S(1)}, u32[32]{0:T(128)}, u32[]{:S(2)}) copy-start(u32[32]{0:T(128)} %constant.351) | copy-start | bytes 388
  654.7 537.9 %reduce-scatter.46.cloned.1.call-start = ((), (), s32[]{:S(2)}) async-start(), calls=%async_computation.32 | async-start | bytes 49152 | tf_op jit(solution)/shard_map/reduce_scatter | solution.py:92
  656.3 548.8 %reduce-scatter.54.cloned.1.call-start = ((), (), s32[]{:S(2)}) async-start(), calls=%async_computation.36 | async-start | bytes 49152 | tf_op jit(solution)/shard_map/reduce_scatter | solution.py:101
  657.8 560.2 %reduce-scatter.50.cloned.1.call-start = ((), (), s32[]{:S(2)}) async-start(), calls=%async_computation.34 | async-start | bytes 196608 | tf_op jit(solution)/shard_map/reduce_scatter | solution.py:98
  672.5 558.4 %reduce-scatter.48.cloned.1.call-start = ((), (), s32[]{:S(2)}) async-start(), calls=%async_computation.33 | async-start | bytes 196608 | tf_op jit(solution)/shard_map/reduce_scatter | solution.py:95
  732.9 510.5 %reduce-scatter.42.cloned.1.call-start = ((), (), s32[]{:S(2)}) async-start(), calls=%async_computation.30 | async-start | bytes 49152 | tf_op jit(solution)/shard_map/reduce_scatter | solution.py:89
  792.7 463.3 %reduce-scatter.30.cloned.1.call-start = ((), (), s32[]{:S(2)}) async-start(), calls=%async_computation.24 | async-start | bytes 49152 | tf_op jit(solution)/shard_map/reduce_scatter | solution.py:80
  853.3 120.4 %copy-start.4 = (f32[1024,512]{0,1:T(8,128)S(1)}, f32[1024,512]{0,1:T(8,128)}, u32[]{:S(2)}) copy-start(f32[1024,512]{0,1:T(8,128)} %copy-done.3) | copy-start | bytes 6291460
  853.3 414.6 %reduce-scatter.38.cloned.1.call-start = ((), (), s32[]{:S(2)}) async-start(), calls=%async_computation.28 | async-start | bytes 49152 | tf_op jit(solution)/shard_map/reduce_scatter | solution.py:86
  913.3 367.2 %reduce-scatter.34.cloned.1.call-start = ((), (), s32[]{:S(2)}) async-start(), calls=%async_computation.26 | async-start | bytes 49152 | tf_op jit(solution)/shard_map/reduce_scatter | solution.py:83
  973.7 319.4 %reduce-scatter.58.cloned.1.call-start = ((), (), s32[]{:S(2)}) async-start(), calls=%async_computation.38 | async-start | bytes 196608 | tf_op jit(solution)/shard_map/reduce_scatter | solution.py:104
  979.8 69.5 %copy-start.22 = (bf16[512,512]{1,0:T(8,128)(2,1)S(1)}, bf16[512,512]{1,0:T(8,128)(2,1)}, u32[]{:S(2)}) copy-start(bf16[512,512]{1,0:T(8,128)(2,1)} %copy-done.21) | copy-start | bytes 1572868
  981.6 143.3 %copy-start.24 = (bf16[512,512]{1,0:T(8,128)(2,1)S(1)}, bf16[512,512]{1,0:T(8,128)(2,1)}, u32[]{:S(2)}) copy-start(bf16[512,512]{1,0:T(8,128)(2,1)} %copy-done.23) | copy-start | bytes 1572868
  981.6 143.3 %copy-start.38 = (bf16[4,344,128]{1,2,0:T(8,128)(2,1)S(1)}, bf16[4,344,128]{1,2,0:T(8,128)(2,1)}, u32[]{:S(2)}) copy-start(bf16[4,344,128]{1,2,0:T(8,128)(2,1)} %get-tuple-element.557) | copy-start | bytes 1056772
  1049.2 256.4 %reduce-scatter.62.cloned.1.call-start = ((), (), s32[]{:S(2)}) async-start(), calls=%async_computation.40 | async-start | bytes 196608 | tf_op jit(solution)/shard_map/reduce_scatter | solution.py:107
  1049.3 257.8 %copy-start.1 = (bf16[1,344,512]{2,1,0:T(8,128)(2,1)S(1)}, bf16[1,344,512]{2,1,0:T(8,128)(2,1)}, u32[]{:S(2)}) copy-start(bf16[1,344,512]{2,1,0:T(8,128)(2,1)} %param.26) | copy-start | bytes 1056772
  (91 other events, 209.4 us)
Sparse Core Ops, SparseCore 0:
  15.1 41.7 all-gather.4
  59.1 41.4 all-gather.6
  495.9 54.5 reduce-scatter.43
  554.5 56.5 reduce-scatter.51
  614.5 56.3 reduce-scatter.65
  674.8 56.4 reduce-scatter.63
  734.9 56.2 reduce-scatter.39
  795.3 56.5 reduce-scatter.27
  855.5 56.3 reduce-scatter.35
  915.7 56.4 reduce-scatter.31
  976.1 71.4 reduce-scatter.55
  1051.8 71.3 reduce-scatter.59
  1126.7 54.3 reduce-scatter.67
  1183.7 8.8 reduce-scatter.45
  1195.2 9.8 reduce-scatter.53
  1207.7 10.2 reduce-scatter.49
  1220.6 10.2 reduce-scatter.47
  1233.5 9.8 reduce-scatter.41
  1246.1 9.8 reduce-scatter.29
  1258.1 9.8 reduce-scatter.37
  1270.7 9.8 reduce-scatter.33
  1282.8 10.2 reduce-scatter.57
  1295.3 10.2 reduce-scatter.61
where the time goes:
time: 1320 us; the launch traced here: 1310 us
  waiting for transfers between devices  595 us (45%)
  blocking collectives  243 us (18%)
  matrix products  182 us (14%)
  local copies, waits for them, and re-layouts  138 us (10%)
  other arithmetic  94.3 us (7%)
  loops' own time  43.9 us (3%)
  between operations  16 us (1%)
    unnamed x26, waiting for transfers between devices  127 us
    reduce_scatter x1, waiting for transfers between devices, reduce_all(): lax.psum_scatter(g_shrink, 'dp', scatter_dimension=0, tiled=True)  72.4 us
    reduce_scatter x1, waiting for transfers between devices, reduce_all(): lax.psum_scatter(g_expand, 'dp', scatter_dimension=0, tiled=True)  66 us
    reduce_scatter x1, waiting for transfers between devices, reduce_all(): lax.psum_scatter(g_sk, 'dp', scatter_dimension=0, tiled=True)  58.8 us
    reduce_scatter x1, waiting for transfers between devices, reduce_all(): lax.psum_scatter(g_so, 'dp', scatter_dimension=0, tiled=True)  58.3 us
    reduce_scatter x1, waiting for transfers between devices, reduce_all(): lax.psum_scatter(g_sq, 'dp', scatter_dimension=0, tiled=True)  57.8 us
    reduce_scatter x1, waiting for transfers between devices, reduce_all(): lax.psum_scatter(g_sv, 'dp', scatter_dimension=0, tiled=True)  49 us
    dot_general x10, matrix products, weight_dot(): lax.dot_general(left, right, (((0,), (0,)), ((), ())), preferred_element_...  36.6 us
  transfers between devices with their start and end apart: 23, of which 19 were waited for; matrix products, arithmetic and copies ran while one was open for 22% of the time, Pallas kernels for 0%

commit v1 on v0

--- a/solution.py
+++ b/solution.py
@@ -1,6 +1,11 @@
+import functools
+
 import jax
 import jax.numpy as jnp
 from jax import lax
+from jax.experimental import pallas as pl
+from jax.experimental.pallas import tpu as pltpu
+from jax.sharding import Mesh
 from jax.sharding import PartitionSpec as P
 
 HEAD_DIM = 64
@@ -33,84 +38,116 @@
     )
 
 
-def gather_all(w_sq, w_sk, w_sv, w_so, w_cq, w_ck, w_cv, w_co, expand, shrink, affine):
-    halves = (
-        lax.all_gather(w_sq, "inner", axis=1, tiled=True),
-        lax.all_gather(w_sk, "inner", axis=1, tiled=True),
-        lax.all_gather(w_sv, "inner", axis=1, tiled=True),
-        lax.all_gather(w_so, "inner", axis=1, tiled=True),
-        lax.all_gather(w_cq, "inner", axis=1, tiled=True),
-        lax.all_gather(w_ck, "inner", axis=1, tiled=True),
-        lax.all_gather(w_cv, "inner", axis=1, tiled=True),
-        lax.all_gather(w_co, "inner", axis=1, tiled=True),
-        lax.all_gather(expand, "inner", axis=1, tiled=True),
-        lax.all_gather(shrink, "inner", axis=1, tiled=True),
-        lax.all_gather(affine, "inner", axis=0, tiled=True),
-    )
-    return (
-        lax.all_gather(halves[0], "dp", axis=0, tiled=True),
-        lax.all_gather(halves[1], "dp", axis=0, tiled=True),
-        lax.all_gather(halves[2], "dp", axis=0, tiled=True),
-        lax.all_gather(halves[3], "dp", axis=0, tiled=True),
-        lax.all_gather(halves[4], "dp", axis=0, tiled=True),
-        lax.all_gather(halves[5], "dp", axis=0, tiled=True),
-        lax.all_gather(halves[6], "dp", axis=0, tiled=True),
-        lax.all_gather(halves[7], "dp", axis=0, tiled=True),
-        lax.all_gather(halves[8], "dp", axis=0, tiled=True),
-        lax.all_gather(halves[9], "dp", axis=0, tiled=True),
-        lax.all_gather(halves[10], "dp", axis=1, tiled=True),
-    )
-
-
-def reduce_all(g_sq, g_sk, g_sv, g_so, g_cq, g_ck, g_cv, g_co, g_expand, g_shrink, g_affine):
-    partial_sums = (
-        lax.psum_scatter(g_sq, "dp", scatter_dimension=0, tiled=True),
-        lax.psum_scatter(g_sk, "dp", scatter_dimension=0, tiled=True),
-        lax.psum_scatter(g_sv, "dp", scatter_dimension=0, tiled=True),
-        lax.psum_scatter(g_so, "dp", scatter_dimension=0, tiled=True),
-        lax.psum_scatter(g_cq, "dp", scatter_dimension=0, tiled=True),
-        lax.psum_scatter(g_ck, "dp", scatter_dimension=0, tiled=True),
-        lax.psum_scatter(g_cv, "dp", scatter_dimension=0, tiled=True),
-        lax.psum_scatter(g_co, "dp", scatter_dimension=0, tiled=True),
-        lax.psum_scatter(g_expand, "dp", scatter_dimension=0, tiled=True),
-        lax.psum_scatter(g_shrink, "dp", scatter_dimension=0, tiled=True),
-        lax.psum_scatter(g_affine, "dp", scatter_dimension=1, tiled=True),
-    )
-    return (
-        lax.psum_scatter(
-            partial_sums[0].astype(jnp.bfloat16), "inner", scatter_dimension=1, tiled=True
-        ).astype(jnp.float32),
-        lax.psum_scatter(
-            partial_sums[1].astype(jnp.bfloat16), "inner", scatter_dimension=1, tiled=True
-        ).astype(jnp.float32),
-        lax.psum_scatter(
-            partial_sums[2].astype(jnp.bfloat16), "inner", scatter_dimension=1, tiled=True
-        ).astype(jnp.float32),
-        lax.psum_scatter(
-            partial_sums[3].astype(jnp.bfloat16), "inner", scatter_dimension=1, tiled=True
-        ).astype(jnp.float32),
-        lax.psum_scatter(
-            partial_sums[4].astype(jnp.bfloat16), "inner", scatter_dimension=1, tiled=True
-        ).astype(jnp.float32),
-        lax.psum_scatter(
-            partial_sums[5].astype(jnp.bfloat16), "inner", scatter_dimension=1, tiled=True
-        ).astype(jnp.float32),
-        lax.psum_scatter(
-            partial_sums[6].astype(jnp.bfloat16), "inner", scatter_dimension=1, tiled=True
-        ).astype(jnp.float32),
-        lax.psum_scatter(
-            partial_sums[7].astype(jnp.bfloat16), "inner", scatter_dimension=1, tiled=True
-        ).astype(jnp.float32),
-        lax.psum_scatter(
-            partial_sums[8].astype(jnp.bfloat16), "inner", scatter_dimension=1, tiled=True
-        ).astype(jnp.float32),
-        lax.psum_scatter(
-            partial_sums[9].astype(jnp.bfloat16), "inner", scatter_dimension=1, tiled=True
-        ).astype(jnp.float32),
-        lax.psum_scatter(
-            partial_sums[10].astype(jnp.bfloat16), "inner", scatter_dimension=0, tiled=True
-        ).astype(jnp.float32),
-    )
+SWAP = [(0, 1), (1, 0)]
+SHIFTS = [[(i, (i + k) % 4) for i in range(4)] for k in range(4)]
+CROSS = [[(i, i ^ k) for i in range(4)] for k in range(4)]
+
+
+def along_line(array):
+    return [array] + [lax.ppermute(array, "a", SHIFTS[k]) for k in (1, 2, 3)]
+
+
+def along_plane(array):
+    return [array] + [lax.ppermute(array, ("b", "i"), CROSS[k]) for k in (1, 2, 3)]
+
+
+def across_cores(arrays):
+    return arrays + [lax.ppermute(array, "c", SWAP) for array in arrays]
+
+
+def fetch_line_first(shard):
+    return across_cores(along_plane(jnp.stack(along_line(shard), 0)))
+
+
+def fetch_plane_first(shard):
+    return across_cores(along_line(jnp.stack(along_plane(shard), 0)))
+
+
+def place_of(coords, line_first, part, entry):
+    core, first = part // 4, part % 4
+    back, plane = (entry, first) if line_first else (first, entry)
+    line = (coords[0] - back) & 3
+    outer = coords[1] ^ (plane >> 1)
+    inner = coords[3] ^ (plane & 1)
+    dp = (line * 2 + outer) * 2 + (coords[2] ^ core)
+    return dp, inner
+
+
+def assemble_kernel(line_first, rows, cols, coords, *refs):
+    pieces, out, sems = refs[:8], refs[8], refs[9]
+    copies = []
+    for part in range(8):
+        for entry in range(4):
+            dp, inner = place_of(coords, line_first, part, entry)
+            spot = out.at[
+                :, pl.ds(pl.multiple_of(dp * rows, rows), rows), pl.ds(pl.multiple_of(inner * cols, cols), cols)
+            ]
+            copy = pltpu.make_async_copy(pieces[part].at[entry], spot, sems.at[part * 4 + entry])
+            copy.start()
+            copies.append(copy)
+    for copy in copies:
+        copy.wait()
+
+
+def assemble(coords, pieces, line_first):
+    _, count, rows, cols = pieces[0].shape
+    return pl.pallas_call(
+        functools.partial(assemble_kernel, line_first, rows, cols),
+        out_shape=jax.ShapeDtypeStruct((count, rows * 16, cols * 2), pieces[0].dtype),
+        in_specs=[pl.BlockSpec(memory_space=pltpu.SMEM)] + [pl.BlockSpec(memory_space=pl.ANY)] * 8,
+        out_specs=pl.BlockSpec(memory_space=pl.ANY),
+        scratch_shapes=[pltpu.SemaphoreType.DMA((32,))],
+        name="assemble",
+    )(coords, *pieces)
+
+
+def pick(array, index, axis):
+    return lax.dynamic_index_in_dim(array, index, axis, keepdims=False)
+
+
+def plane_block(array, coords, step, cols):
+    outer = coords[1] ^ (step >> 1)
+    inner = coords[3] ^ (step & 1)
+    array = pick(array, outer, array.ndim - 3)
+    return lax.dynamic_slice_in_dim(array, inner * cols, cols, array.ndim - 1)
+
+
+def spread_line(total, coords, axis):
+    mine = pick(total, coords[0], axis)
+    for k in (1, 2, 3):
+        block = pick(total, (coords[0] + k) & 3, axis).astype(jnp.bfloat16)
+        mine = mine + lax.ppermute(block, "a", SHIFTS[k]).astype(jnp.float32)
+    return mine
+
+
+def spread_plane(total, coords, cols):
+    mine = plane_block(total, coords, 0, cols)
+    for k in (1, 2, 3):
+        block = plane_block(total, coords, k, cols).astype(jnp.bfloat16)
+        mine = mine + lax.ppermute(block, ("b", "i"), CROSS[k]).astype(jnp.float32)
+    return mine
+
+
+def reduce_group(grads, coords, rest, plane_first=True):
+    count, rows, cols = grads.shape
+    shard, half = rows // 16, cols // 2
+    blocks = grads.reshape(count, 4, 2, 2, shard, cols)
+    away = pick(blocks, 1 - coords[2], 3).astype(jnp.bfloat16)
+    total = pick(blocks, coords[2], 3).astype(jnp.float32)
+    total = total + lax.ppermute(away, "c", SWAP).astype(jnp.float32)
+    if plane_first:
+        total = spread_line(spread_plane(total, coords, half), coords, 1)
+    else:
+        total = spread_plane(spread_line(total, coords, 1), coords, half)
+    if rest > 1:
+        total = lax.psum_scatter(total, "r", scatter_dimension=1, tiled=True)
+    return total
+
+
+def sum_all(array):
+    for names, perms in (("c", [SWAP]), (("b", "i"), CROSS[1:]), ("a", SHIFTS[1:])):
+        array = sum([lax.ppermute(array, names, perm) for perm in perms], array)
+    return array
 
 
 def pair_mask(query_segs, key_segs, keep_row):
@@ -262,20 +299,28 @@
     rows, length, width = target.shape
     src_length = source.shape[1]
     tokens = rows * length
-    fetched = gather_all(
-        self_query,
-        self_key,
-        self_value,
-        self_output,
-        cross_query,
-        cross_key,
-        cross_value,
-        cross_output,
-        expand_weight,
-        shrink_weight,
-        norm_affine,
-    )
-    w_sq, w_sk, w_sv, w_so, w_cq, w_ck, w_cv, w_co, expand, shrink, affine_low = fetched
+    coords = jnp.stack([lax.axis_index(name) for name in "abci"]).astype(jnp.int32)
+    rest = lax.axis_size("r")
+
+    def whole_rows(shard):
+        return lax.all_gather(shard, "r", axis=1, tiled=True) if rest > 1 else shard
+
+    shard_one = whole_rows(jnp.stack([self_query, self_key, self_value]))
+    shard_two = whole_rows(jnp.stack([self_output, cross_query, cross_key, cross_value, cross_output]))
+    shard_three = whole_rows(expand_weight[None])
+    shard_four = whole_rows(shrink_weight[None])
+    w_sq, w_sk, w_sv = assemble(coords, fetch_line_first(shard_one), True)
+    w_so, w_cq, w_ck, w_cv, w_co = assemble(coords, fetch_line_first(shard_two), True)
+    expand = assemble(coords, fetch_plane_first(shard_three), False)[0]
+    shrink = assemble(coords, fetch_line_first(shard_four), True)[0]
+    wide = norm_affine.shape[1]
+    column = (((coords[0] * 2 + coords[1]) * 2 + coords[2]) * rest + lax.axis_index("r")) * wide
+    affine_low = lax.dynamic_update_slice(
+        jnp.zeros((6, width), jnp.float32), norm_affine.astype(jnp.float32), (coords[3] * 3, column)
+    )
+    if rest > 1:
+        affine_low = lax.psum(affine_low, "r")
+    affine_low = sum_all(affine_low)
     affine = affine_low.astype(jnp.float32)
     all_keep = jnp.ones_like(target_segment)
     stream = target.reshape(tokens, width).astype(jnp.float32)
@@ -304,20 +349,8 @@
     active, gelu_pull = jax.vjp(jax.nn.gelu, hidden)
     active = active.astype(jnp.bfloat16)
     result = (second_sum + forward_dot(active, shrink)).astype(jnp.bfloat16)
-    refetched = gather_all(
-        self_query,
-        self_key,
-        self_value,
-        self_output,
-        cross_query,
-        cross_key,
-        cross_value,
-        cross_output,
-        expand_weight,
-        shrink_weight,
-        norm_affine,
-    )
-    b_sq, b_sk, b_sv, b_so, b_cq, b_ck, b_cv, b_co, b_expand, b_shrink, b_affine = refetched
+    b_sq, b_sk, b_sv, b_so, b_cq, b_ck, b_cv, b_co = w_sq, w_sk, w_sv, w_so, w_cq, w_ck, w_cv, w_co
+    b_expand, b_shrink = expand, shrink
     out_back = cotangent.reshape(tokens, width)
     shrink_grad = weight_dot(active, out_back)
     active_back = input_dot(out_back, b_shrink)
@@ -367,19 +400,16 @@
     stream_ln, gain_one, bias_one = norm_one_pull(normed_one_back)
     stream_back = first_back + stream_ln
     affine_grad = jnp.stack([gain_one, bias_one, gain_two, bias_two, gain_three, bias_three], 0)
-    reduced = reduce_all(
-        self_query_grad,
-        self_key_grad,
-        self_value_grad,
-        self_out_grad,
-        cross_query_grad,
-        cross_key_grad,
-        cross_value_grad,
-        cross_out_grad,
-        expand_grad,
-        shrink_grad,
-        affine_grad,
-    )
+    g_shrink = reduce_group(shrink_grad[None], coords, rest, False)[0]
+    g_expand = reduce_group(expand_grad[None], coords, rest)[0]
+    g_two = reduce_group(
+        jnp.stack([self_out_grad, cross_query_grad, cross_key_grad, cross_value_grad, cross_out_grad]), coords, rest
+    )
+    g_one = reduce_group(jnp.stack([self_query_grad, self_key_grad, self_value_grad]), coords, rest)
+    if rest > 1:
+        affine_grad = lax.psum(affine_grad, "r")
+    g_affine = lax.dynamic_slice(sum_all(affine_grad), (coords[3] * 3, column), (3, wide))
+    reduced = (*g_one, *g_two, g_expand, g_shrink, g_affine)
     return (
         result.reshape(rows, length, width),
         stream_back.reshape(rows, length, width),
@@ -399,39 +429,42 @@
 
 
 def solution(mesh):
+    dp, inner = mesh.shape["dp"], mesh.shape["inner"]
+    fine = Mesh(mesh.devices.reshape(4, 2, 2, dp // 16, inner), ("a", "b", "c", "r", "i"))
+    split = ("a", "b", "c", "r")
     in_specs = (
-        P(("dp", "inner"), None, None),
-        P(("dp", "inner"), None, None),
-        P(("dp", "inner"), None),
-        P(("dp", "inner"), None),
-        P(("dp", "inner"), None),
-        P("dp", "inner"),
-        P("dp", "inner"),
-        P("dp", "inner"),
-        P("dp", "inner"),
-        P("dp", "inner"),
-        P("dp", "inner"),
-        P("dp", "inner"),
-        P("dp", "inner"),
-        P("dp", "inner"),
-        P("dp", "inner"),
-        P("inner", "dp"),
-        P(("dp", "inner"), None, None),
+        P((*split, "i"), None, None),
+        P((*split, "i"), None, None),
+        P((*split, "i"), None),
+        P((*split, "i"), None),
+        P((*split, "i"), None),
+        P(split, "i"),
+        P(split, "i"),
+        P(split, "i"),
+        P(split, "i"),
+        P(split, "i"),
+        P(split, "i"),
+        P(split, "i"),
+        P(split, "i"),
+        P(split, "i"),
+        P(split, "i"),
+        P("i", split),
+        P((*split, "i"), None, None),
     )
     out_specs = (
-        P(("dp", "inner"), None, None),
-        P(("dp", "inner"), None, None),
-        P(("dp", "inner"), None, None),
-        P("dp", "inner"),
-        P("dp", "inner"),
-        P("dp", "inner"),
-        P("dp", "inner"),
-        P("dp", "inner"),
-        P("dp", "inner"),
-        P("dp", "inner"),
-        P("dp", "inner"),
-        P("dp", "inner"),
-        P("dp", "inner"),
-        P("inner", "dp"),
-    )
-    return jax.shard_map(shards, mesh=mesh, in_specs=in_specs, out_specs=out_specs, check_vma=False)
+        P((*split, "i"), None, None),
+        P((*split, "i"), None, None),
+        P((*split, "i"), None, None),
+        P(split, "i"),
+        P(split, "i"),
+        P(split, "i"),
+        P(split, "i"),
+        P(split, "i"),
+        P(split, "i"),
+        P(split, "i"),
+        P(split, "i"),
+        P(split, "i"),
+        P(split, "i"),
+        P("i", split),
+    )
+    return jax.shard_map(shards, mesh=fine, in_specs=in_specs, out_specs=out_specs, check_vma=False)

time: 1320 us -> 816 us (0.62)
  waiting for transfers between devices: 595 us -> 53.3 us
  Pallas kernels: 0 us -> 262 us
  blocking collectives: 243 us -> 0 us
  starting transfers between devices: 1.59 us -> 90.7 us
  other arithmetic: 94.3 us -> 72.7 us
  matrix products: 182 us -> 163 us
  local copies, waits for them, and re-layouts: 138 us -> 120 us
  between operations: 16 us -> 2.53 us
    reduce_scatter x18 -> x0, waiting for transfers between devices: 468 us -> none  [the longest x1 72.4 us: reduce_all(): lax.psum_scatter(g_shrink, 'dp', scatter_dimension=0, tiled=True)]
    pallas_call x0 -> x4, Pallas kernels: none -> 262 us  [assemble(): pl.pallas_call(functools.partial(assemble_kernel, line_first, rows, cols)...]
    all_gather x20 -> x0, blocking collectives: 238 us -> none  [the longest x1 21.8 us: gather_all(): lax.all_gather(halves[10], 'dp', axis=1, tiled=True)]
    unnamed x26 -> x0, waiting for transfers between devices: 127 us -> none
    ppermute x0 -> x82, starting transfers between devices: none -> 90.7 us  [the longest x12 23.6 us: spread_line(): mine = mine + lax.ppermute(block, 'a', SHIFTS[k]).astype(jnp.float32)]
    ppermute x0 -> x82, waiting for transfers between devices: none -> 53.3 us  [the longest x12 18.1 us: spread_plane(): mine = mine + lax.ppermute(block, ('b', 'i'), CROSS[k]).astype(jnp.float32)]
    convert_element_type x18 -> x1, other arithmetic: 23.6 us -> 0.68 us  [shards(): norm_affine.astype(jnp.float32)]
    dot_general x10, matrix products: 36.6 us -> 23 us  [weight_dot(): lax.dot_general(left, right, (((0,), (0,)), ((), ())), preferred_element_...]
  transfers between devices with their start and end apart: 23 -> 82, of which waited for: 19 -> 22; matrix products, arithmetic and copies ran while one was open for 22% -> 24% of each run, Pallas kernels for 0% -> 22%
where the time goes in v1:
time: 816 us; the launch traced here: 808 us
  Pallas kernels  262 us (32%)
  matrix products  163 us (20%)
  local copies, waits for them, and re-layouts  120 us (15%)
  starting transfers between devices  90.7 us (11%)
  other arithmetic  72.7 us (9%)
  waiting for transfers between devices  53.3 us (7%)
  loops' own time  44.5 us (5%)
    pallas_call x4, Pallas kernels, assemble(): pl.pallas_call(functools.partial(assemble_kernel, line_first, rows, cols)...  262 us
    dot_general x10, matrix products, forward_dot(): return jnp.dot(left, weight, preferred_element_type=jnp.float32)  28.7 us
    another operation x2, loops' own time, attend_back(): lax.map(one_pair, jnp.arange(rows * pairs, dtype=jnp.int32))  27.6 us
    dot_general x10, matrix products, input_dot(): lax.dot_general(upstream, weight, (((1,), (1,)), ((), ())), preferred_ele...  26.7 us
    dot_general x32, matrix products, pair_scores(): jnp.einsum('qhd,khd->hqk', query_block, key_rows, preferred_element_type=...  24 us
    ppermute x12, starting transfers between devices, spread_line(): mine = mine + lax.ppermute(block, 'a', SHIFTS[k]).astype(jnp.float32)  23.6 us
    dynamic_slice x24, local copies, waits for them, and re-layouts, slice_pair(): piece = lax.dynamic_slice(array, (row, 0, column), (1, count, 2 * HEAD_DIM))  23 us
    dot_general x10, matrix products, weight_dot(): lax.dot_general(left, right, (((0,), (0,)), ((), ())), preferred_element_...  23 us
  transfers between devices with their start and end apart: 82, of which 22 were waited for; matrix products, arithmetic and copies ran while one was open for 24% of the time, Pallas kernels for 22%

profile of v1, /device:TPU:0, one launch (start us, length us, event | category | flops | bytes accessed | tf_op | source)
XLA Modules:
  0.0 808.3 jit_solution(2033938230373477912)
XLA Ops:
  1.6 4.1 collective-permute-start.8
  11.3 2.9 collective-permute-start.3
  33.5 2.4 collective-permute-start.19
  42.2 5.1 collective-permute-done.18
  52.4 2.7 collective-permute-done.10.refs_1_
  55.7 5.6 collective-permute-done.42.refs_3_
  61.3 2.5 collective-permute-done.41.refs_2_
  71.0 49.7 %assemble.4 = bf16[3,512,512]{2,1,0:T(8,128)(2,1)} custom-call(s32[4]{0:T(128)} %pad_add_fusion.coords, bf16[4,3,32,256]{3,2,1,0:T(8,128)(2,1)} %copy-done.49, bf16[4,3,32,256]{3,2,1,0:T(8,128)(2,1)} %copy-done.56, bf16[4,3,32,256]{3,2,1,0:T(8,128)(2,1)} %copy-done.55, bf16[4,3,32,256]{3,2,1,0:T(8,128)(2,1)} %copy-done.54, ...), custom_call_target="tpu_custom_call" | custom-call | tf_op jit(solution)/shard_map/assemble/pallas_call | solution.py:94
  120.7 2.8 fusion.96
  124.6 2.8 fusion.97
  130.3 3.1 fusion.95
  138.3 51.0 %while.60 = (s32[]{:T(128)}, bf16[4,1024,128]{1,2,0:T(8,128)(2,1)}, f32[4,2,1024]{2,1,0:T(2,128)S(1)}, s32[4]{0:T(128)S(1)}, bf16[1,1024,512]{1,2,0:T(8,128)(2,1...) while((s32[]{:T(128)}, bf16[4,1024,128]{1,2,0:T(8,128)(2,1)}, ...), condition=%wide.region_7.8_spmd, body=%wide.region_2.7_spmd.sunk | while | flops 563609600 | bytes 33128796 | solution.py:211
  189.3 65.6 %assemble.7 = bf16[1,2048,512]{2,1,0:T(8,128)(2,1)} custom-call(s32[4]{0:T(128)} %pad_add_fusion.coords, bf16[4,1,128,256]{3,2,1,0:T(8,128)(2,1)} %copy-done.41, bf16[4,1,128,256]{3,2,1,0:T(8,128)(2,1)} %collective-permute-done.40.refs_1_, bf16[4,1,128,256]{3,2,1,0:T(8,128)(2,1)} %collective-permute-done.41.refs_2_, ...), custom_call_target="tpu_custom_call" | custom-call | tf_op jit(solution)/shard_map/assemble/pallas_call | solution.py:94
  254.9 65.6 %assemble.6 = bf16[1,512,2048]{2,1,0:T(8,128)(2,1)} custom-call(s32[4]{0:T(128)} %pad_add_fusion.coords, bf16[4,1,32,1024]{3,2,1,0:T(8,128)(2,1)} %copy-done.42, bf16[4,1,32,1024]{3,2,1,0:T(8,128)(2,1)} %copy-done.52, bf16[4,1,32,1024]{3,2,1,0:T(8,128)(2,1)} %collective-permute-done.31.refs_2_, bf16[4,1,32,1024]{3,2,1,0:T(8,128)(2,1)} %collective-permute-done.32.refs_3_, ...), custom_call_target="tpu_custom_call" | custom-call | tf_op jit(solution)/shard_map/assemble/pallas_call | solution.py:94
  320.6 81.5 %assemble.5 = bf16[5,512,512]{2,1,0:T(8,128)(2,1)} custom-call(s32[4]{0:T(128)} %pad_add_fusion.coords, bf16[4,5,32,256]{3,2,1,0:T(8,128)(2,1)} %copy-done.38, bf16[4,5,32,256]{3,2,1,0:T(8,128)(2,1)} %collective-permute-done.20.refs_1_, bf16[4,5,32,256]{3,2,1,0:T(8,128)(2,1)} %collective-permute-done.21.refs_2_, ...), custom_call_target="tpu_custom_call" | custom-call | tf_op jit(solution)/shard_map/assemble/pallas_call | solution.py:94
  414.0 34.4 %while.61 = (s32[]{:T(128)}, bf16[4,1024,128]{1,2,0:T(8,128)(2,1)S(1)}, f32[4,2,1024]{2,1,0:T(2,128)S(1)}, s32[4]{0:T(128)S(1)}, bf16[1,344,512]{1,2,0:T(8,128)(...) while((s32[]{:T(128)}, ...), condition=%wide.region_15.16_spmd, body=%wide.region_10.15_spmd.sunk | while | flops 187220320 | bytes 11536984 | solution.py:211
  453.0 6.6 fusion.62
  459.6 4.7 fusion.89
  464.3 7.6 fusion.54
  471.9 4.3 fusion.197
  476.1 4.6 fusion.182
  480.7 2.9 copy.41
  483.6 3.6 multiply_reduce_fusion.4
  489.1 3.1 fusion.99
  493.4 60.5 %while.62 = (s32[]{:T(128)}, bf16[4,1024,128]{1,2,0:T(8,128)(2,1)}, bf16[4,344,128]{1,2,0:T(8,128)(2,1)}, bf16[4,344,128]{1,2,0:T(8,128)(2,1)}, s32[4]{0:T(128)S...) while((s32[]{:T(128)}, bf16[4,1024,128]{1,2,0:T(8,128)(2,1)}, ...), condition=%wide.region_23.24_spmd, body=%wide.region_20.23_spmd.sunk | while | flops 458937696 | bytes 28506832 | solution.py:272
  555.4 2.5 fusion.132
  557.9 6.6 copy.94
  564.6 6.9 fusion.109
  573.7 2.8 fusion.106
  576.5 2.7 fusion.107
  583.5 3.1 fusion.196
  586.6 2.9 copy.46
  599.3 91.8 %while.63 = (s32[]{:T(128)}, bf16[4,1024,128]{1,2,0:T(8,128)(2,1)}, bf16[4,1024,128]{1,2,0:T(8,128)(2,1)}, bf16[4,1024,128]{1,2,0:T(8,128)(2,1)S(1)}, s32[4]{0:T...) while((s32[]{:T(128)}, bf16[4,1024,128]{1,2,0:T(8,128)(2,1)}, ...), condition=%wide.region_29.30_spmd, body=%wide.region_26.29_spmd.sunk | while | flops 1376122880 | bytes 76898712 | solution.py:272
  709.7 2.5 add_bitcast_fusion
  713.9 3.0 copy.75
  725.9 4.3 collective-permute-done.48
  730.2 3.3 collective-permute-start.81
  738.2 3.6 collective-permute-start.53
  744.1 2.7 collective-permute-done.52
  755.1 3.1 collective-permute-done.62
  759.1 2.7 collective-permute-done.64
  763.5 3.8 collective-permute-start.67
  768.3 8.7 %collective-permute-start.66 = (bf16[1,32,1024]{2,1,0:T(8,128)(2,1)S(1)}, bf16[1,32,1024]{2,1,0:T(8,128)(2,1)S(1)}, u32[]{:S(2)}, u32[]{:S(2)}) collective-permute-start(bf16[1,32,1024]{2,1,0:T(8,128)(2,1)S(1)} %get-tuple-element.784), channel_id=1, source_target_pairs={{0,16},{8,24},{16,0},{24,8},{1,17},{9,25},{17,1},{25,9},{2,18},{10... | collective-permute-start | bytes 196616 | tf_op jit(solution)/shard_map/ppermute | solution.py:119
  778.8 3.5 collective-permute-done.70
  789.8 3.5 collective-permute-done.57
  793.3 4.5 collective-permute-done.56
  798.2 3.8 collective-permute-start.60
  804.5 2.8 collective-permute-done.59
  (824 shorter events, 344.2 us)
Async XLA Ops:
  1.6 27.8 %collective-permute-start.8 = (bf16[3,32,256]{2,1,0:T(8,128)(2,1)S(1)}, bf16[3,32,256]{2,1,0:T(8,128)(2,1)S(1)}, u32[]{:S(2)}, u32[]{:S(2)}) collective-permute-start(bf16[3,32,256]{2,1,0:T(8,128)(2,1)S(1)} %get-tuple-element.797), channel_id=1, source_target_pairs={{0,16},{8,24},{16,0},{24,8},{1,17},{9,25},{17,1},{25,9},{2,18},{10... | collective-permute-start | bytes 147464 | tf_op jit(solution)/shard_map/ppermute | solution.py:47
  5.7 25.3 %collective-permute-start.7 = (bf16[3,32,256]{2,1,0:T(8,128)(2,1)S(1)}, bf16[3,32,256]{2,1,0:T(8,128)(2,1)S(1)}, u32[]{:S(2)}, u32[]{:S(2)}) collective-permute-start(bf16[3,32,256]{2,1,0:T(8,128)(2,1)S(1)} %get-tuple-element.797), channel_id=1, source_target_pairs={{0,8},{8,16},{16,24},{24,0},{1,9},{9,17},{17,25},{25,1},{2,10},{10... | collective-permute-start | bytes 147464 | tf_op jit(solution)/shard_map/ppermute | solution.py:47
  16.0 16.0 %collective-permute-start.9 = (bf16[3,32,256]{2,1,0:T(8,128)(2,1)S(1)}, bf16[3,32,256]{2,1,0:T(8,128)(2,1)S(1)}, u32[]{:S(2)}, u32[]{:S(2)}) collective-permute-start(bf16[3,32,256]{2,1,0:T(8,128)(2,1)S(1)} %get-tuple-element.797), channel_id=1, source_target_pairs={{0,24},{8,0},{16,8},{24,16},{1,25},{9,1},{17,9},{25,17},{2,26},{10... | collective-permute-start | bytes 147464 | tf_op jit(solution)/shard_map/ppermute | solution.py:47
  36.0 12.0 %collective-permute-start.13 = (bf16[4,3,32,256]{3,2,1,0:T(8,128)(2,1)S(1)}, bf16[4,3,32,256]{3,2,1,0:T(8,128)(2,1)S(1)}, u32[]{:S(2)}, u32[]{:S(2)}) collective-permute-start(bf16[4,3,32,256]{3,2,1,0:T(8,128)(2,1)S(1)} %pad_maximum_fusion.4.refs_0_), channel_id=1, source_target_pairs={{0,2},{2,0},{1,3},{3,1},{4,6},{6,4},{5,7},{7,5},{8,10},{10,8},{9,1... | collective-permute-start | bytes 589832 | tf_op jit(solution)/shard_map/ppermute | solution.py:55
  36.0 13.9 %collective-permute-start.12 = (bf16[4,3,32,256]{3,2,1,0:T(8,128)(2,1)S(1)}, bf16[4,3,32,256]{3,2,1,0:T(8,128)(2,1)S(1)}, u32[]{:S(2)}, u32[]{:S(2)}) collective-permute-start(bf16[4,3,32,256]{3,2,1,0:T(8,128)(2,1)S(1)} %pad_maximum_fusion.4.refs_0_), channel_id=1, source_target_pairs={{0,5},{1,4},{4,1},{5,0},{2,7},{3,6},{6,3},{7,2},{8,13},{9,12},{12,... | collective-permute-start | bytes 589832 | tf_op jit(solution)/shard_map/ppermute | solution.py:51
  38.7 12.2 %collective-permute-start.11 = (bf16[4,3,32,256]{3,2,1,0:T(8,128)(2,1)S(1)}, bf16[4,3,32,256]{3,2,1,0:T(8,128)(2,1)S(1)}, u32[]{:S(2)}, u32[]{:S(2)}) collective-permute-start(bf16[4,3,32,256]{3,2,1,0:T(8,128)(2,1)S(1)} %pad_maximum_fusion.4.refs_0_), channel_id=1, source_target_pairs={{0,4},{1,5},{4,0},{5,1},{2,6},{3,7},{6,2},{7,3},{8,12},{9,13},{12,... | collective-permute-start | bytes 589832 | tf_op jit(solution)/shard_map/ppermute | solution.py:51
  48.0 13.4 %collective-permute-start.42 = (bf16[4,1,128,256]{3,2,1,0:T(8,128)(2,1)S(1)}, bf16[4,1,128,256]{3,2,1,0:T(8,128)(2,1)}, u32[]{:S(2)}, u32[]{:S(2)}) collective-permute-start(bf16[4,1,128,256]{3,2,1,0:T(8,128)(2,1)S(1)} %pad_maximum_fusion.3.refs_0_), channel_id=1, source_target_pairs={{0,5},{1,4},{4,1},{5,0},{2,7},{3,6},{6,3},{7,2},{8,13},{9,12},{12,... | collective-permute-start | bytes 786440 | tf_op jit(solution)/shard_map/ppermute | solution.py:51
  49.9 14.0 %collective-permute-start.41 = (bf16[4,1,128,256]{3,2,1,0:T(8,128)(2,1)S(1)}, bf16[4,1,128,256]{3,2,1,0:T(8,128)(2,1)}, u32[]{:S(2)}, u32[]{:S(2)}) collective-permute-start(bf16[4,1,128,256]{3,2,1,0:T(8,128)(2,1)S(1)} %pad_maximum_fusion.3.refs_0_), channel_id=1, source_target_pairs={{0,4},{1,5},{4,0},{5,1},{2,6},{3,7},{6,2},{7,3},{8,12},{9,13},{12,... | collective-permute-start | bytes 786440 | tf_op jit(solution)/shard_map/ppermute | solution.py:51
  50.9 14.5 %collective-permute-start.40 = (bf16[4,1,128,256]{3,2,1,0:T(8,128)(2,1)S(1)}, bf16[4,1,128,256]{3,2,1,0:T(8,128)(2,1)}, u32[]{:S(2)}, u32[]{:S(2)}) collective-permute-start(bf16[4,1,128,256]{3,2,1,0:T(8,128)(2,1)S(1)} %pad_maximum_fusion.3.refs_0_), channel_id=1, source_target_pairs={{0,1},{1,0},{4,5},{5,4},{2,3},{3,2},{6,7},{7,6},{8,9},{9,8},{12,13... | collective-permute-start | bytes 786440 | tf_op jit(solution)/shard_map/ppermute | solution.py:51
  55.1 11.0 %collective-permute-start.33 = (bf16[4,1,32,1024]{3,2,1,0:T(8,128)(2,1)S(1)}, bf16[4,1,32,1024]{3,2,1,0:T(8,128)(2,1)S(1)}, u32[]{:S(2)}, u32[]{:S(2)}) collective-permute-start(bf16[4,1,32,1024]{3,2,1,0:T(8,128)(2,1)S(1)} %pad_maximum_fusion.2.refs_0_), channel_id=1, source_target_pairs={{0,2},{2,0},{1,3},{3,1},{4,6},{6,4},{5,7},{7,5},{8,10},{10,8},{9,1... | collective-permute-start | bytes 786440 | tf_op jit(solution)/shard_map/ppermute | solution.py:55
  55.1 11.1 %collective-permute-start.32 = (bf16[4,1,32,1024]{3,2,1,0:T(8,128)(2,1)S(1)}, bf16[4,1,32,1024]{3,2,1,0:T(8,128)(2,1)}, u32[]{:S(2)}, u32[]{:S(2)}) collective-permute-start(bf16[4,1,32,1024]{3,2,1,0:T(8,128)(2,1)S(1)} %pad_maximum_fusion.2.refs_0_), channel_id=1, source_target_pairs={{0,24},{8,0},{16,8},{24,16},{1,25},{9,1},{17,9},{25,17},{2,26},{10... | collective-permute-start | bytes 786440 | tf_op jit(solution)/shard_map/ppermute | solution.py:47
  66.1 57.4 %collective-permute-start.31 = (bf16[4,1,32,1024]{3,2,1,0:T(8,128)(2,1)S(1)}, bf16[4,1,32,1024]{3,2,1,0:T(8,128)(2,1)}, u32[]{:S(2)}, u32[]{:S(2)}) collective-permute-start(bf16[4,1,32,1024]{3,2,1,0:T(8,128)(2,1)S(1)} %pad_maximum_fusion.2.refs_0_), channel_id=1, source_target_pairs={{0,16},{8,24},{16,0},{24,8},{1,17},{9,25},{17,1},{25,9},{2,18},{10... | collective-permute-start | bytes 786440 | tf_op jit(solution)/shard_map/ppermute | solution.py:47
  66.2 57.3 %collective-permute-start.30 = (bf16[4,1,32,1024]{3,2,1,0:T(8,128)(2,1)S(1)}, bf16[4,1,32,1024]{3,2,1,0:T(8,128)(2,1)S(1)}, u32[]{:S(2)}, u32[]{:S(2)}) collective-permute-start(bf16[4,1,32,1024]{3,2,1,0:T(8,128)(2,1)S(1)} %pad_maximum_fusion.2.refs_0_), channel_id=1, source_target_pairs={{0,8},{8,16},{16,24},{24,0},{1,9},{9,17},{17,25},{25,1},{2,10},{10... | collective-permute-start | bytes 786440 | tf_op jit(solution)/shard_map/ppermute | solution.py:47
  67.0 57.0 %collective-permute-start.22 = (bf16[4,5,32,256]{3,2,1,0:T(8,128)(2,1)S(1)}, bf16[4,5,32,256]{3,2,1,0:T(8,128)(2,1)}, u32[]{:S(2)}, u32[]{:S(2)}) collective-permute-start(bf16[4,5,32,256]{3,2,1,0:T(8,128)(2,1)S(1)} %pad_maximum_fusion.1.refs_0_), channel_id=1, source_target_pairs={{0,5},{1,4},{4,1},{5,0},{2,7},{3,6},{6,3},{7,2},{8,13},{9,12},{12,... | collective-permute-start | bytes 983048 | tf_op jit(solution)/shard_map/ppermute | solution.py:51
  68.3 55.8 %collective-permute-start.21 = (bf16[4,5,32,256]{3,2,1,0:T(8,128)(2,1)S(1)}, bf16[4,5,32,256]{3,2,1,0:T(8,128)(2,1)}, u32[]{:S(2)}, u32[]{:S(2)}) collective-permute-start(bf16[4,5,32,256]{3,2,1,0:T(8,128)(2,1)S(1)} %pad_maximum_fusion.1.refs_0_), channel_id=1, source_target_pairs={{0,4},{1,5},{4,0},{5,1},{2,6},{3,7},{6,2},{7,3},{8,12},{9,13},{12,... | collective-permute-start | bytes 983048 | tf_op jit(solution)/shard_map/ppermute | solution.py:51
  69.4 55.1 %collective-permute-start.20 = (bf16[4,5,32,256]{3,2,1,0:T(8,128)(2,1)S(1)}, bf16[4,5,32,256]{3,2,1,0:T(8,128)(2,1)}, u32[]{:S(2)}, u32[]{:S(2)}) collective-permute-start(bf16[4,5,32,256]{3,2,1,0:T(8,128)(2,1)S(1)} %pad_maximum_fusion.1.refs_0_), channel_id=1, source_target_pairs={{0,1},{1,0},{4,5},{5,4},{2,3},{3,2},{6,7},{7,6},{8,9},{9,8},{12,13... | collective-permute-start | bytes 983048 | tf_op jit(solution)/shard_map/ppermute | solution.py:51
  123.5 12.2 %collective-permute-start.46 = (bf16[4,1,128,256]{3,2,1,0:T(8,128)(2,1)}, bf16[4,1,128,256]{3,2,1,0:T(8,128)(2,1)}, u32[]{:S(2)}, u32[]{:S(2)}) collective-permute-start(bf16[4,1,128,256]{3,2,1,0:T(8,128)(2,1)} %collective-permute-done.42.refs_3_), channel_id=1, source_target_pairs={{0,2},{2,0},{1,3},{3,1},{4,6},{6,4},{5,7},{7,5},{8,10},{10,8},{9,1... | collective-permute-start | bytes 786440 | tf_op jit(solution)/shard_map/ppermute | solution.py:55
  123.5 12.6 %collective-permute-start.45 = (bf16[4,1,128,256]{3,2,1,0:T(8,128)(2,1)}, bf16[4,1,128,256]{3,2,1,0:T(8,128)(2,1)}, u32[]{:S(2)}, u32[]{:S(2)}) collective-permute-start(bf16[4,1,128,256]{3,2,1,0:T(8,128)(2,1)} %collective-permute-done.41.refs_2_), channel_id=1, source_target_pairs={{0,2},{2,0},{1,3},{3,1},{4,6},{6,4},{5,7},{7,5},{8,10},{10,8},{9,1... | collective-permute-start | bytes 786440 | tf_op jit(solution)/shard_map/ppermute | solution.py:55
  124.0 12.2 %collective-permute-start.44 = (bf16[4,1,128,256]{3,2,1,0:T(8,128)(2,1)}, bf16[4,1,128,256]{3,2,1,0:T(8,128)(2,1)}, u32[]{:S(2)}, u32[]{:S(2)}) collective-permute-start(bf16[4,1,128,256]{3,2,1,0:T(8,128)(2,1)} %collective-permute-done.40.refs_1_), channel_id=1, source_target_pairs={{0,2},{2,0},{1,3},{3,1},{4,6},{6,4},{5,7},{7,5},{8,10},{10,8},{9,1... | collective-permute-start | bytes 786440 | tf_op jit(solution)/shard_map/ppermute | solution.py:55
  124.1 12.6 %collective-permute-start.36 = (bf16[4,1,32,1024]{3,2,1,0:T(8,128)(2,1)}, bf16[4,1,32,1024]{3,2,1,0:T(8,128)(2,1)}, u32[]{:S(2)}, u32[]{:S(2)}) collective-permute-start(bf16[4,1,32,1024]{3,2,1,0:T(8,128)(2,1)} %collective-permute-done.32.refs_3_), channel_id=1, source_target_pairs={{0,2},{2,0},{1,3},{3,1},{4,6},{6,4},{5,7},{7,5},{8,10},{10,8},{9,1... | collective-permute-start | bytes 786440 | tf_op jit(solution)/shard_map/ppermute | solution.py:55
  124.5 12.2 %collective-permute-start.35 = (bf16[4,1,32,1024]{3,2,1,0:T(8,128)(2,1)}, bf16[4,1,32,1024]{3,2,1,0:T(8,128)(2,1)}, u32[]{:S(2)}, u32[]{:S(2)}) collective-permute-start(bf16[4,1,32,1024]{3,2,1,0:T(8,128)(2,1)} %collective-permute-done.31.refs_2_), channel_id=1, source_target_pairs={{0,2},{2,0},{1,3},{3,1},{4,6},{6,4},{5,7},{7,5},{8,10},{10,8},{9,1... | collective-permute-start | bytes 786440 | tf_op jit(solution)/shard_map/ppermute | solution.py:55
  135.7 184.8 %collective-permute-start.23 = (bf16[4,5,32,256]{3,2,1,0:T(8,128)(2,1)}, bf16[4,5,32,256]{3,2,1,0:T(8,128)(2,1)}, u32[]{:S(2)}, u32[]{:S(2)}) collective-permute-start(bf16[4,5,32,256]{3,2,1,0:T(8,128)(2,1)} %copy-done.38), channel_id=1, source_target_pairs={{0,2},{2,0},{1,3},{3,1},{4,6},{6,4},{5,7},{7,5},{8,10},{10,8},{9,1... | collective-permute-start | bytes 983048 | tf_op jit(solution)/shard_map/ppermute | solution.py:55
  136.1 118.8 %collective-permute-start.34 = (bf16[4,1,32,1024]{3,2,1,0:T(8,128)(2,1)}, bf16[4,1,32,1024]{3,2,1,0:T(8,128)(2,1)}, u32[]{:S(2)}, u32[]{:S(2)}) collective-permute-start(bf16[4,1,32,1024]{3,2,1,0:T(8,128)(2,1)} %copy-done.52), channel_id=1, source_target_pairs={{0,2},{2,0},{1,3},{3,1},{4,6},{6,4},{5,7},{7,5},{8,10},{10,8},{9,1... | collective-permute-start | bytes 786440 | tf_op jit(solution)/shard_map/ppermute | solution.py:55
  136.2 184.3 %collective-permute-start.26 = (bf16[4,5,32,256]{3,2,1,0:T(8,128)(2,1)}, bf16[4,5,32,256]{3,2,1,0:T(8,128)(2,1)}, u32[]{:S(2)}, u32[]{:S(2)}) collective-permute-start(bf16[4,5,32,256]{3,2,1,0:T(8,128)(2,1)} %collective-permute-done.22.refs_3_), channel_id=1, source_target_pairs={{0,2},{2,0},{1,3},{3,1},{4,6},{6,4},{5,7},{7,5},{8,10},{10,8},{9,1... | collective-permute-start | bytes 983048 | tf_op jit(solution)/shard_map/ppermute | solution.py:55
  136.6 183.9 %collective-permute-start.25 = (bf16[4,5,32,256]{3,2,1,0:T(8,128)(2,1)}, bf16[4,5,32,256]{3,2,1,0:T(8,128)(2,1)}, u32[]{:S(2)}, u32[]{:S(2)}) collective-permute-start(bf16[4,5,32,256]{3,2,1,0:T(8,128)(2,1)} %collective-permute-done.21.refs_2_), channel_id=1, source_target_pairs={{0,2},{2,0},{1,3},{3,1},{4,6},{6,4},{5,7},{7,5},{8,10},{10,8},{9,1... | collective-permute-start | bytes 983048 | tf_op jit(solution)/shard_map/ppermute | solution.py:55
  136.7 183.8 %collective-permute-start.24 = (bf16[4,5,32,256]{3,2,1,0:T(8,128)(2,1)}, bf16[4,5,32,256]{3,2,1,0:T(8,128)(2,1)}, u32[]{:S(2)}, u32[]{:S(2)}) collective-permute-start(bf16[4,5,32,256]{3,2,1,0:T(8,128)(2,1)} %collective-permute-done.20.refs_1_), channel_id=1, source_target_pairs={{0,2},{2,0},{1,3},{3,1},{4,6},{6,4},{5,7},{7,5},{8,10},{10,8},{9,1... | collective-permute-start | bytes 983048 | tf_op jit(solution)/shard_map/ppermute | solution.py:55
  579.2 168.3 %collective-permute-start.61 = (bf16[1,4,2,32,2048]{4,3,1,2,0:T(8,128)(2,1)}, bf16[1,4,2,32,2048]{4,3,1,2,0:T(8,128)(2,1)}, u32[]{:S(2)}, u32[]{:S(2)}) collective-permute-start(bf16[1,4,2,32,2048]{4,3,1,2,0:T(8,128)(2,1)} %fusion.107), channel_id=1, source_target_pairs={{0,2},{2,0},{1,3},{3,1},{4,6},{6,4},{5,7},{7,5},{8,10},{10,8},{9,1... | collective-permute-start | bytes 3145736 | tf_op jit(solution)/shard_map/ppermute | solution.py:137
  579.3 173.8 %collective-permute-start.68 = (bf16[1,4,2,128,512]{4,3,2,1,0:T(8,128)(2,1)}, bf16[1,4,2,128,512]{4,3,2,1,0:T(8,128)(2,1)}, u32[]{:S(2)}, u32[]{:S(2)}) collective-permute-start(bf16[1,4,2,128,512]{4,3,2,1,0:T(8,128)(2,1)} %fusion.106), channel_id=1, source_target_pairs={{0,2},{2,0},{1,3},{3,1},{4,6},{6,4},{5,7},{7,5},{8,10},{10,8},{9,1... | collective-permute-start | bytes 3145736 | tf_op jit(solution)/shard_map/ppermute | solution.py:137
  696.7 22.7 %collective-permute-start.47 = (bf16[3,4,2,32,512]{4,3,2,1,0:T(8,128)(2,1)}, bf16[3,4,2,32,512]{4,3,2,1,0:T(8,128)(2,1)}, u32[]{:S(2)}, u32[]{:S(2)}) collective-permute-start(bf16[3,4,2,32,512]{4,3,2,1,0:T(8,128)(2,1)} %fusion.116), channel_id=1, source_target_pairs={{0,2},{2,0},{1,3},{3,1},{4,6},{6,4},{5,7},{7,5},{8,10},{10,8},{9,1... | collective-permute-start | bytes 2359304 | tf_op jit(solution)/shard_map/ppermute | solution.py:137
  703.7 13.2 %collective-permute-start.75 = (f32[6,512]{1,0:T(8,128)S(1)}, f32[6,512]{1,0:T(8,128)S(1)}, u32[]{:S(2)}, u32[]{:S(2)}) collective-permute-start(f32[6,512]{1,0:T(8,128)S(1)} %stack.163), channel_id=1, source_target_pairs={{0,2},{2,0},{1,3},{3,1},{4,6},{6,4},{5,7},{7,5},{8,10},{10,8},{9,1... | collective-permute-start | bytes 36872 | tf_op jit(solution)/shard_map/ppermute | solution.py:149
  723.4 10.1 %collective-permute-start.50 = (bf16[3,4,32,256]{3,2,1,0:T(8,128)(2,1)S(1)}, bf16[3,4,32,256]{3,2,1,0:T(8,128)(2,1)S(1)}, u32[]{:S(2)}, u32[]{:S(2)}) collective-permute-start(bf16[3,4,32,256]{3,2,1,0:T(8,128)(2,1)S(1)} %get-tuple-element.774), channel_id=1, source_target_pairs={{0,5},{1,4},{4,1},{5,0},{2,7},{3,6},{6,3},{7,2},{8,13},{9,12},{12,... | collective-permute-start | bytes 589832 | tf_op jit(solution)/shard_map/ppermute | solution.py:127
  724.7 11.2 %collective-permute-start.49 = (bf16[3,4,32,256]{3,2,1,0:T(8,128)(2,1)S(1)}, bf16[3,4,32,256]{3,2,1,0:T(8,128)(2,1)S(1)}, u32[]{:S(2)}, u32[]{:S(2)}) collective-permute-start(bf16[3,4,32,256]{3,2,1,0:T(8,128)(2,1)S(1)} %get-tuple-element.775), channel_id=1, source_target_pairs={{0,4},{1,5},{4,0},{5,1},{2,6},{3,7},{6,2},{7,3},{8,12},{9,13},{12,... | collective-permute-start | bytes 589832 | tf_op jit(solution)/shard_map/ppermute | solution.py:127
  743.9 19.6 %collective-permute-start.54 = (bf16[5,4,2,32,512]{4,3,2,1,0:T(8,128)(2,1)S(1)}, bf16[5,4,2,32,512]{4,3,2,1,0:T(8,128)(2,1)S(1)}, u32[]{:S(2)}, u32[]{:S(2)}) collective-permute-start(bf16[5,4,2,32,512]{4,3,2,1,0:T(8,128)(2,1)S(1)} %copy-done.37), channel_id=1, source_target_pairs={{0,2},{2,0},{1,3},{3,1},{4,6},{6,4},{5,7},{7,5},{8,10},{10,8},{9,1... | collective-permute-start | bytes 3932168 | tf_op jit(solution)/shard_map/ppermute | solution.py:137
  749.5 8.7 %collective-permute-start.62 = (bf16[1,4,32,1024]{3,2,1,0:T(8,128)(2,1)S(1)}, bf16[1,4,32,1024]{3,2,1,0:T(8,128)(2,1)S(1)}, u32[]{:S(2)}, u32[]{:S(2)}) collective-permute-start(bf16[1,4,32,1024]{3,2,1,0:T(8,128)(2,1)S(1)} %get-tuple-element.770), channel_id=1, source_target_pairs={{0,1},{1,0},{4,5},{5,4},{2,3},{3,2},{6,7},{7,6},{8,9},{9,8},{12,13... | collective-permute-start | bytes 786440 | tf_op jit(solution)/shard_map/ppermute | solution.py:127
  751.0 10.8 %collective-permute-start.64 = (bf16[1,4,32,1024]{3,2,1,0:T(8,128)(2,1)S(1)}, bf16[1,4,32,1024]{3,2,1,0:T(8,128)(2,1)S(1)}, u32[]{:S(2)}, u32[]{:S(2)}) collective-permute-start(bf16[1,4,32,1024]{3,2,1,0:T(8,128)(2,1)S(1)} %get-tuple-element.771), channel_id=1, source_target_pairs={{0,5},{1,4},{4,1},{5,0},{2,7},{3,6},{6,3},{7,2},{8,13},{9,12},{12,... | collective-permute-start | bytes 786440 | tf_op jit(solution)/shard_map/ppermute | solution.py:127
  752.2 11.0 %collective-permute-start.63 = (bf16[1,4,32,1024]{3,2,1,0:T(8,128)(2,1)S(1)}, bf16[1,4,32,1024]{3,2,1,0:T(8,128)(2,1)S(1)}, u32[]{:S(2)}, u32[]{:S(2)}) collective-permute-start(bf16[1,4,32,1024]{3,2,1,0:T(8,128)(2,1)S(1)} %get-tuple-element.772), channel_id=1, source_target_pairs={{0,4},{1,5},{4,0},{5,1},{2,6},{3,7},{6,2},{7,3},{8,12},{9,13},{12,... | collective-permute-start | bytes 786440 | tf_op jit(solution)/shard_map/ppermute | solution.py:127
  754.8 13.5 %collective-permute-start.69 = (bf16[1,2,128,512]{3,2,1,0:T(8,128)(2,1)S(1)}, bf16[1,2,128,512]{3,2,1,0:T(8,128)(2,1)S(1)}, u32[]{:S(2)}, u32[]{:S(2)}) collective-permute-start(bf16[1,2,128,512]{3,2,1,0:T(8,128)(2,1)S(1)} %get-tuple-element.767), channel_id=1, source_target_pairs={{0,8},{8,16},{16,24},{24,0},{1,9},{9,17},{17,25},{25,1},{2,10},{10... | collective-permute-start | bytes 786440 | tf_op jit(solution)/shard_map/ppermute | solution.py:119
  758.3 18.8 %collective-permute-start.71 = (bf16[1,2,128,512]{3,2,1,0:T(8,128)(2,1)S(1)}, bf16[1,2,128,512]{3,2,1,0:T(8,128)(2,1)S(1)}, u32[]{:S(2)}, u32[]{:S(2)}) collective-permute-start(bf16[1,2,128,512]{3,2,1,0:T(8,128)(2,1)S(1)} %get-tuple-element.768), channel_id=1, source_target_pairs={{0,24},{8,0},{16,8},{24,16},{1,25},{9,1},{17,9},{25,17},{2,26},{10... | collective-permute-start | bytes 786440 | tf_op jit(solution)/shard_map/ppermute | solution.py:119
  761.7 20.6 %collective-permute-start.70 = (bf16[1,2,128,512]{3,2,1,0:T(8,128)(2,1)S(1)}, bf16[1,2,128,512]{3,2,1,0:T(8,128)(2,1)S(1)}, u32[]{:S(2)}, u32[]{:S(2)}) collective-permute-start(bf16[1,2,128,512]{3,2,1,0:T(8,128)(2,1)S(1)} %get-tuple-element.769), channel_id=1, source_target_pairs={{0,16},{8,24},{16,0},{24,8},{1,17},{9,25},{17,1},{25,9},{2,18},{10... | collective-permute-start | bytes 786440 | tf_op jit(solution)/shard_map/ppermute | solution.py:119
  763.5 20.3 %collective-permute-start.65 = (bf16[1,32,1024]{2,1,0:T(8,128)(2,1)S(1)}, bf16[1,32,1024]{2,1,0:T(8,128)(2,1)S(1)}, u32[]{:S(2)}, u32[]{:S(2)}) collective-permute-start(bf16[1,32,1024]{2,1,0:T(8,128)(2,1)S(1)} %get-tuple-element.782), channel_id=1, source_target_pairs={{0,8},{8,16},{16,24},{24,0},{1,9},{9,17},{17,25},{25,1},{2,10},{10... | collective-permute-start | bytes 196616 | tf_op jit(solution)/shard_map/ppermute | solution.py:119
  763.5 22.1 %collective-permute-start.67 = (bf16[1,32,1024]{2,1,0:T(8,128)(2,1)S(1)}, bf16[1,32,1024]{2,1,0:T(8,128)(2,1)S(1)}, u32[]{:S(2)}, u32[]{:S(2)}) collective-permute-start(bf16[1,32,1024]{2,1,0:T(8,128)(2,1)S(1)} %get-tuple-element.783), channel_id=1, source_target_pairs={{0,24},{8,0},{16,8},{24,16},{1,25},{9,1},{17,9},{25,17},{2,26},{10... | collective-permute-start | bytes 196616 | tf_op jit(solution)/shard_map/ppermute | solution.py:119
  768.3 18.0 %collective-permute-start.66 = (bf16[1,32,1024]{2,1,0:T(8,128)(2,1)S(1)}, bf16[1,32,1024]{2,1,0:T(8,128)(2,1)S(1)}, u32[]{:S(2)}, u32[]{:S(2)}) collective-permute-start(bf16[1,32,1024]{2,1,0:T(8,128)(2,1)S(1)} %get-tuple-element.784), channel_id=1, source_target_pairs={{0,16},{8,24},{16,0},{24,8},{1,17},{9,25},{17,1},{25,9},{2,18},{10... | collective-permute-start | bytes 196616 | tf_op jit(solution)/shard_map/ppermute | solution.py:119
  777.1 11.2 %collective-permute-start.55 = (bf16[5,4,32,256]{3,2,1,0:T(8,128)(2,1)S(1)}, bf16[5,4,32,256]{3,2,1,0:T(8,128)(2,1)S(1)}, u32[]{:S(2)}, u32[]{:S(2)}) collective-permute-start(bf16[5,4,32,256]{3,2,1,0:T(8,128)(2,1)S(1)} %get-tuple-element.764), channel_id=1, source_target_pairs={{0,1},{1,0},{4,5},{5,4},{2,3},{3,2},{6,7},{7,6},{8,9},{9,8},{12,13... | collective-permute-start | bytes 983048 | tf_op jit(solution)/shard_map/ppermute | solution.py:127
  782.4 10.9 %collective-permute-start.57 = (bf16[5,4,32,256]{3,2,1,0:T(8,128)(2,1)S(1)}, bf16[5,4,32,256]{3,2,1,0:T(8,128)(2,1)S(1)}, u32[]{:S(2)}, u32[]{:S(2)}) collective-permute-start(bf16[5,4,32,256]{3,2,1,0:T(8,128)(2,1)S(1)} %get-tuple-element.765), channel_id=1, source_target_pairs={{0,5},{1,4},{4,1},{5,0},{2,7},{3,6},{6,3},{7,2},{8,13},{9,12},{12,... | collective-permute-start | bytes 983048 | tf_op jit(solution)/shard_map/ppermute | solution.py:127
  783.8 14.0 %collective-permute-start.56 = (bf16[5,4,32,256]{3,2,1,0:T(8,128)(2,1)S(1)}, bf16[5,4,32,256]{3,2,1,0:T(8,128)(2,1)S(1)}, u32[]{:S(2)}, u32[]{:S(2)}) collective-permute-start(bf16[5,4,32,256]{3,2,1,0:T(8,128)(2,1)S(1)} %get-tuple-element.766), channel_id=1, source_target_pairs={{0,4},{1,5},{4,0},{5,1},{2,6},{3,7},{6,2},{7,3},{8,12},{9,13},{12,... | collective-permute-start | bytes 983048 | tf_op jit(solution)/shard_map/ppermute | solution.py:127
  785.6 16.4 %collective-permute-start.72 = (bf16[1,128,256]{2,1,0:T(8,128)(2,1)S(1)}, bf16[1,128,256]{2,1,0:T(8,128)(2,1)S(1)}, u32[]{:S(2)}, u32[]{:S(2)}) collective-permute-start(bf16[1,128,256]{2,1,0:T(8,128)(2,1)S(1)} %get-tuple-element.779), channel_id=1, source_target_pairs={{0,1},{1,0},{4,5},{5,4},{2,3},{3,2},{6,7},{7,6},{8,9},{9,8},{12,13... | collective-permute-start | bytes 196616 | tf_op jit(solution)/shard_map/ppermute | solution.py:127
  786.3 15.7 %collective-permute-start.74 = (bf16[1,128,256]{2,1,0:T(8,128)(2,1)S(1)}, bf16[1,128,256]{2,1,0:T(8,128)(2,1)S(1)}, u32[]{:S(2)}, u32[]{:S(2)}) collective-permute-start(bf16[1,128,256]{2,1,0:T(8,128)(2,1)S(1)} %get-tuple-element.780), channel_id=1, source_target_pairs={{0,5},{1,4},{4,1},{5,0},{2,7},{3,6},{6,3},{7,2},{8,13},{9,12},{12,... | collective-permute-start | bytes 196616 | tf_op jit(solution)/shard_map/ppermute | solution.py:127
  788.2 13.8 %collective-permute-start.73 = (bf16[1,128,256]{2,1,0:T(8,128)(2,1)S(1)}, bf16[1,128,256]{2,1,0:T(8,128)(2,1)S(1)}, u32[]{:S(2)}, u32[]{:S(2)}) collective-permute-start(bf16[1,128,256]{2,1,0:T(8,128)(2,1)S(1)} %get-tuple-element.781), channel_id=1, source_target_pairs={{0,4},{1,5},{4,0},{5,1},{2,6},{3,7},{6,2},{7,3},{8,12},{9,13},{12,... | collective-permute-start | bytes 196616 | tf_op jit(solution)/shard_map/ppermute | solution.py:127
  (148 other events, 2459.4 us)
